TPU v7x, 32 devices: a whole 2x2x4 slice. The times are simulated.
32 devices in a mesh: grp: 2 (over core), row: 4 (over y, x), col: 4 (over z).
Axes of the slice: x: 2, y: 2, z: 4, core: 2. Of those that a mesh axis runs over, the one named last changes fastest.
Arguments:
- velocity: bfloat16 [3, 64, 16, 512], P(None, None, ('row', 'col'), 'grp'), may hold values from -0.25 to 0.25
- density: float32 [64, 16, 2048], P(('row', 'col'), None, 'grp'), may hold values from -6 to 6
- live_planes: int32 [16], P(('row', 'col')), may hold values from 1 to 4, 32 in all
Outputs:
- density_next: float32 [64, 16, 2048], P(('row', 'col'), None, 'grp')
- buoyancy: float32 [64, 16, 512], P(None, ('row', 'col'), 'grp')
Inputs may be any that keep to these rules, and one draw needn't show every extreme that they name: live_planes[s] counts the planes of slab s, from its first plane on, that are advanced; the counts sum to 32 and one of them equals 4.
All inputs are finite; a program needn't handle non-finite values. No bound on the sum of `live_planes` on one device may be relied on, other than what follows from the above.
Results may differ from a plain program's by a relative error of at most 0.0035.
Values may be sent and summed in bfloat16 or wider, within the bound.
No kernel may reach another device: no remote copies, remote signals or barrier semaphores. Data moves between devices by JAX's collectives and lax.ppermute only.
A program may use at most 128 MiB of HBM per device.

v0:
```python
import math

import jax
import jax.numpy as jnp
from jax import lax
from jax.sharding import PartitionSpec as P

first_coef = (4.0 / 5.0, -1.0 / 5.0, 4.0 / 105.0, -1.0 / 280.0)
second_coef = (8.0 / 5.0, -1.0 / 5.0, 8.0 / 315.0, -1.0 / 560.0)
centre_coef = -205.0 / 72.0
kappa_value = 0.1
step_value = 0.2
strat_value = 1.0


def with_halo(block, sides, width):
    for axis, dim in sides:
        count = lax.axis_size(axis)
        forward = [(i, i + 1) for i in range(count - 1)]
        forward.append((count - 1, 0))
        backward = [(target, source) for source, target in forward]
        low = lax.ppermute(
            lax.slice_in_dim(block, block.shape[dim] - width, None, axis=dim), axis, forward
        )
        high = lax.ppermute(lax.slice_in_dim(block, 0, width, axis=dim), axis, backward)
        block = jnp.concatenate([low, block, high], axis=dim)
    return block


def basis_rows(mode_count, fine_cells, first_cell, cell_count):
    index_k = jnp.arange(mode_count, dtype=jnp.int32)
    index_i = first_cell + jnp.arange(cell_count, dtype=jnp.int32)
    half_modes = mode_count // 2
    frequency = jnp.where(index_k < half_modes, index_k, index_k - half_modes + 1)
    phase = frequency[:, None] * index_i[None, :] % fine_cells
    angle = phase.astype(jnp.float32) * (2.0 * math.pi / fine_cells)
    table = jnp.where((index_k < half_modes)[:, None], jnp.cos(angle), jnp.sin(angle))
    return table.astype(jnp.bfloat16)


def tendency(field, along_x, along_z, fine_velocity):
    plane_count = field.shape[0]
    cell_count = field.shape[2]
    grad_x = jnp.zeros_like(field)
    grad_y = jnp.zeros_like(field)
    grad_z = jnp.zeros_like(field)
    laplace = 3.0 * centre_coef * field
    for reach in range(1, 5):
        ahead = along_x[:, :, 4 + reach : 4 + reach + cell_count]
        behind = along_x[:, :, 4 - reach : 4 - reach + cell_count]
        grad_x = grad_x + first_coef[reach - 1] * (ahead - behind)
        laplace = laplace + second_coef[reach - 1] * (ahead + behind)
        ahead = jnp.roll(field, -reach, axis=1)
        behind = jnp.roll(field, reach, axis=1)
        grad_y = grad_y + first_coef[reach - 1] * (ahead - behind)
        laplace = laplace + second_coef[reach - 1] * (ahead + behind)
        ahead = along_z[4 + reach : 4 + reach + plane_count]
        behind = along_z[4 - reach : 4 - reach + plane_count]
        grad_z = grad_z + first_coef[reach - 1] * (ahead - behind)
        laplace = laplace + second_coef[reach - 1] * (ahead + behind)
    vel_u = fine_velocity[0]
    vel_v = fine_velocity[1]
    vel_w = fine_velocity[2]
    advect = vel_u * grad_x + vel_v * grad_y + vel_w * grad_z
    return kappa_value * laplace - advect - strat_value * vel_w


def per_device(velocity, density, live_planes):
    mode_count = 2 * velocity.shape[3]
    plane_count, row_count, half_cells = density.shape
    fine_cells = 2 * half_cells
    core_side = lax.axis_index("grp")
    table = basis_rows(mode_count, fine_cells, core_side * half_cells, half_cells)
    received = lax.all_to_all(velocity, ("row", "col"), split_axis=1, concat_axis=2, tiled=True)
    blank = jnp.zeros(received.shape[:3] + (half_cells,), jnp.float32)
    shard_piece = lax.all_gather(received, "grp", axis=3, tiled=True)
    count_here = shard_piece.shape[3]
    product = jnp.dot(
        shard_piece.reshape(-1, count_here), table, preferred_element_type=jnp.float32
    )
    fine_velocity = product.reshape(blank.shape)
    padded = with_halo(density, (("grp", 2), (("row", "col"), 0)), 4)
    along_x = padded[4 : 4 + plane_count]
    along_z = padded[:, :, 4 : 4 + half_cells]
    change = tendency(density, along_x, along_z, fine_velocity)
    active = (jnp.arange(plane_count, dtype=jnp.int32) < live_planes[0])[:, None, None]
    density_next = jnp.where(active, density + step_value * change, density)
    coarse_density = density_next.astype(jnp.bfloat16)
    partial_value = lax.dot_general(
        coarse_density.reshape(-1, half_cells),
        table,
        (((1,), (1,)), ((), ())),
        preferred_element_type=jnp.float32,
    )
    partial_value = partial_value.reshape(plane_count, row_count, mode_count)
    summed = lax.psum_scatter(partial_value, "grp", scatter_dimension=2, tiled=True)
    at_home = lax.all_to_all(summed, ("row", "col"), split_axis=1, concat_axis=0, tiled=True)
    buoyancy = -math.sqrt(2.0 / fine_cells) * at_home
    return (density_next, buoyancy)


def solution(mesh):
    in_specs = (
        P(None, None, ("row", "col"), "grp"),
        P(("row", "col"), None, "grp"),
        P(("row", "col")),
    )
    out_specs = (P(("row", "col"), None, "grp"), P(None, ("row", "col"), "grp"))
    return jax.shard_map(
        per_device, mesh=mesh, in_specs=in_specs, out_specs=out_specs, check_vma=False
    )
```

profile of v0, /device:TPU:0, one launch (start us, length us, event | category | flops | bytes accessed | tf_op | source)
XLA Modules:
  0.0 87.6 jit_solution(8428279392464782983)
XLA Ops:
  7.2 0.9 %fusion.30 = (f32[4,16,4]{2,1,0:T(8,128)S(1)}, f32[4,16,4]{2,1,0:T(8,128)S(1)}) fusion(f32[4,16,1024]{2,1,0:T(8,128)} %param.4), kind=kLoop, calls=%fused_computation.71 | loop fusion | bytes 4096 | tf_op jit(solution)/shard_map/slice | solution.py:25
  8.1 0.5 collective-permute-start
  8.5 0.1 collective-permute-start.1
  8.6 1.6 %copy.12 = bf16[3,64,1,256]{3,0,2,1:T(4,128)(2,1)} copy(bf16[3,64,1,256]{3,1,2,0:T(8,128)(2,1)} %param.3) | data formatting | bytes 196608 | tf_op args[0]
  10.2 8.3 %all-to-all-start = ((bf16[3,64,1,256]{3,0,2,1:T(4,128)(2,1)}), bf16[3,64,1,256]{3,0,2,1:T(4,128)(2,1)}, u32[]{:S(2)}, u32[]{:S(2)}) async-start(bf16[3,64,1,256]{3,0,2,1:T(4,128)(2,1)} %copy.12), calls=%async_computation | async-start | bytes 262144 | tf_op jit(solution)/shard_map/all_to_all | solution.py:74
  18.6 0.0 reduce-scatter.2.cloned.1.call-start
  18.6 0.6 add_select_fusion.2
  19.2 0.6 iota_compare_fusion
  20.0 0.7 fusion.27
  20.7 0.7 fusion.29
  21.4 0.7 fusion.25
  22.0 0.6 fusion.23
  22.7 0.6 iota_add_fusion
  23.9 0.5 iota_compare_fusion.1
  24.4 0.0 collective-permute-done
  24.4 0.0 collective-permute-done.1
  24.4 0.6 copy-done.10
  25.0 0.6 copy-done.6
  25.6 0.2 concatenate.62
  25.8 5.5 %collective-permute-start.2 = (f32[4,16,1032]{2,1,0:T(8,128)S(1)}, f32[4,16,1032]{2,1,0:T(8,128)S(1)}, u32[]{:S(2)}, u32[]{:S(2)}) collective-permute-start(f32[4,16,1032]{2,1,0:T(8,128)S(1)} %concatenate.62), channel_id=1, source_target_pairs={{1,0},{2,1},{3,2},{4,3},{5,4},{6,5},{7,6},{8,7},{9,8},{10,9},{11,1... | collective-permute-start | bytes 792584 | tf_op jit(solution)/shard_map/ppermute | solution.py:25
  31.4 0.0 collective-permute-start.3
  31.4 0.8 constant_dynamic-update-slice_fusion
  32.1 0.0 all-to-all-done
  32.1 0.0 copy-start.15
  32.2 0.9 %copy.18 = bf16[3,16,4,1,256]{4,2,1,0,3:T(4,128)(2,1)S(1)} copy(bf16[3,16,4,1,256]{4,0,2,1,3:T(4,128)(2,1)} %bitcast.1) | data formatting | bytes 196608 | tf_op jit(solution)/shard_map/all_to_all | solution.py:74
  33.1 1.9 %all-gather = bf16[3,4,16,1,512]{4,1,2,0,3:T(4,128)(2,1)S(1)} all-gather(bf16[3,4,16,1,256]{4,1,2,0,3:T(4,128)(2,1)S(1)} %bitcast.25), channel_id=2, replica_groups=mesh['grp'=2,'row'=4,'col'=4] {'grp'}, dimensions={4}, use_global_device_ids=true | all-gather | bytes 294912 | tf_op jit(solution)/shard_map/all_gather | solution.py:76
  35.1 8.6 %convolution_bitcast_fusion = f32[192,1024]{1,0:T(8,128)S(1)} fusion(bf16[192,512]{1,0:T(8,128)(2,1)S(1)} %bitcast.26, s32[1024]{0:T(1024)S(1)} %copy-done.12, s32[512]{0:T(512)S(1)} %copy-done.13, pred[512]{0:T(512)(128)(4,1)S(1)} %copy-done.15), kind=kOutput, calls=%fused_computation.9 | convolution fusion | flops 209715200 | bytes 989696 | tf_op jit(solution)/shard_map/dot_general | solution.py:78
  43.7 0.0 copy-start.3
  43.7 0.0 copy-start.4
  43.7 0.0 copy-start.7
  43.7 0.0 copy-start.8
  43.7 0.0 copy-start.9
  43.8 0.0 copy-start.11
  43.8 0.0 copy-start.14
  43.8 0.1 fusion.21
  43.8 0.0 collective-permute-done.2
  43.9 0.8 collective-permute-done.3
  44.7 0.0 copy-done.3
  44.7 0.0 copy-done.4
  44.7 1.3 %add_select_fusion.1 = f32[4,16,1024]{2,1,0:T(8,128)S(1)} fusion(f32[4,16,1024]{2,1,0:T(8,128)S(1)} %copy-done, f32[4,16,1024]{2,1,0:T(8,128)S(1)} %bitcast.23, f32[4,16,1024]{2,1,0:T(8,128)S(1)} %bitcast.24, f32[4,16,1024]{2,1,0:T(8,128)S(1)} %bitcast.22, f32[4,16,1032]{2,1,0:T(8,128)S(1)} %collective-permute-done.3, ...), kind=kLoop, calls=%fused_computation.23 | loop fusion | flops 6488064 | bytes 6259200 | tf_op jit(solution)/shard_map/jit(_where)/select_n | solution.py:87
  46.0 0.0 copy-start.5
  46.0 0.7 copy-done.5
  46.7 9.5 %fusion.3 = f32[4,16,512]{2,1,0:T(8,128)} fusion(s32[1024]{0:T(1024)S(1)} %copy-done.12, s32[512]{0:T(512)S(1)} %copy-done.13, pred[512]{0:T(512)(128)(4,1)S(1)} %copy-done.15, f32[4,16,1024]{2,1,0:T(8,128)S(1)} %add_select_fusion.1), kind=kOutput, calls=%fused_computation.10 | convolution fusion | flops 75563008 | bytes 399872 | tf_op jit(solution)/shard_map/dot_general | solution.py:89
  56.2 0.0 reduce-scatter.2.cloned.1.call-update
  56.2 9.0 %reduce-scatter.2.cloned.1.call-done = f32[4,16,256]{2,1,0:T(8,128)} async-done(((f32[4,16,512]{2,1,0:T(8,128)}), f32[4,16,256]{2,1,0:T(8,128)}) %reduce-scatter.2.cloned.1.call-update) | async-done | bytes 65552 | tf_op jit(solution)/shard_map/reduce_scatter | solution.py:96
  65.2 0.9 %copy.15 = f32[4,16,256]{2,0,1:T(4,128)S(1)} copy(f32[4,16,256]{2,1,0:T(8,128)} %reduce-scatter.2.cloned.1.call-done) | data formatting | bytes 131072 | tf_op jit(solution)/shard_map/reduce_scatter | solution.py:96
  66.1 14.0 %all_to_all.27 = f32[4,16,256]{2,0,1:T(4,128)S(1)} all-to-all(f32[4,16,256]{2,0,1:T(4,128)S(1)} %copy.15), channel_id=1, replica_groups=mesh['grp'=2,'row'=4,'col'=4] {'row','col'}, dimensions={1} | all-to-all | bytes 131072 | tf_op jit(solution)/shard_map/all_to_all | solution.py:97
  80.1 0.7 mul.187
  (25 shorter events, 0.2 us)
Async XLA Ops:
  7.2 12.7 %copy-start = (f32[4,16,1024]{2,1,0:T(8,128)S(1)}, f32[4,16,1024]{2,1,0:T(8,128)}, u32[]{:S(2)}) copy-start(f32[4,16,1024]{2,1,0:T(8,128)} %param.4) | copy-start | bytes 786436
  8.1 16.4 %collective-permute-start = (f32[4,16,4]{2,1,0:T(8,128)S(1)}, f32[4,16,4]{2,1,0:T(8,128)S(1)}, u32[]{:S(2)}, u32[]{:S(2)}) collective-permute-start(f32[4,16,4]{2,1,0:T(8,128)S(1)} %get-tuple-element.21), channel_id=1, source_target_pairs={{16,0},{0,16},{17,1},{1,17},{18,2},{2,18},{19,3},{3,19},{20,4},{4,... | collective-permute-start | bytes 3080 | tf_op jit(solution)/shard_map/ppermute | solution.py:25
  8.5 15.9 %collective-permute-start.1 = (f32[4,16,4]{2,1,0:T(8,128)S(1)}, f32[4,16,4]{2,1,0:T(8,128)S(1)}, u32[]{:S(2)}, u32[]{:S(2)}) collective-permute-start(f32[4,16,4]{2,1,0:T(8,128)S(1)} %get-tuple-element.22), channel_id=1, source_target_pairs={{0,16},{16,0},{1,17},{17,1},{2,18},{18,2},{3,19},{19,3},{4,20},{20... | collective-permute-start | bytes 3080 | tf_op jit(solution)/shard_map/ppermute | solution.py:22
  10.2 21.9 %all-to-all-start = ((bf16[3,64,1,256]{3,0,2,1:T(4,128)(2,1)}), bf16[3,64,1,256]{3,0,2,1:T(4,128)(2,1)}, u32[]{:S(2)}, u32[]{:S(2)}) async-start(bf16[3,64,1,256]{3,0,2,1:T(4,128)(2,1)} %copy.12), calls=%async_computation | async-start | bytes 262144 | tf_op jit(solution)/shard_map/all_to_all | solution.py:74
  18.6 46.6 %reduce-scatter.2.cloned.1.call-start = ((), (), s32[]{:S(2)}) async-start(), calls=%async_computation.3 | async-start | bytes 196608 | tf_op jit(solution)/shard_map/reduce_scatter | solution.py:96
  24.4 0.6 copy-start.10
  25.0 0.6 copy-start.6
  25.8 18.0 %collective-permute-start.2 = (f32[4,16,1032]{2,1,0:T(8,128)S(1)}, f32[4,16,1032]{2,1,0:T(8,128)S(1)}, u32[]{:S(2)}, u32[]{:S(2)}) collective-permute-start(f32[4,16,1032]{2,1,0:T(8,128)S(1)} %concatenate.62), channel_id=1, source_target_pairs={{1,0},{2,1},{3,2},{4,3},{5,4},{6,5},{7,6},{8,7},{9,8},{10,9},{11,1... | collective-permute-start | bytes 792584 | tf_op jit(solution)/shard_map/ppermute | solution.py:25
  31.4 13.3 %collective-permute-start.3 = (f32[4,16,1032]{2,1,0:T(8,128)S(1)}, f32[4,16,1032]{2,1,0:T(8,128)S(1)}, u32[]{:S(2)}, u32[]{:S(2)}) collective-permute-start(f32[4,16,1032]{2,1,0:T(8,128)S(1)} %concatenate.62), channel_id=1, source_target_pairs={{0,1},{1,2},{2,3},{3,4},{4,5},{5,6},{6,7},{7,8},{8,9},{9,10},{10,1... | collective-permute-start | bytes 792584 | tf_op jit(solution)/shard_map/ppermute | solution.py:22
  32.1 3.0 %copy-start.12 = (s32[1024]{0:T(1024)S(1)}, s32[1024]{0:T(1024)}, u32[]{:S(2)}) copy-start(s32[1024]{0:T(1024)} %iota_add_fusion) | copy-start | bytes 12292
  32.1 3.0 %copy-start.13 = (s32[512]{0:T(512)S(1)}, s32[512]{0:T(512)}, u32[]{:S(2)}) copy-start(s32[512]{0:T(512)} %add_select_fusion.2) | copy-start | bytes 6148
  32.1 3.0 %copy-start.15 = (pred[512]{0:T(512)(128)(4,1)S(1)}, pred[512]{0:T(512)(128)(4,1)}, u32[]{:S(2)}) copy-start(pred[512]{0:T(512)(128)(4,1)} %iota_compare_fusion) | copy-start | bytes 1540
  43.7 1.0 %copy-start.1 = (f32[4,3,1024]{2,1,0:T(4,128)S(1)}, f32[4,3,1024]{2,1,0:T(4,128)}, u32[]{:S(2)}) copy-start(f32[4,3,1024]{2,1,0:T(4,128)} %get-tuple-element.15) | copy-start | bytes 147460
  43.7 1.0 %copy-start.2 = (f32[4,3,1024]{2,1,0:T(4,128)S(1)}, f32[4,3,1024]{2,1,0:T(4,128)}, u32[]{:S(2)}) copy-start(f32[4,3,1024]{2,1,0:T(4,128)} %get-tuple-element.16) | copy-start | bytes 147460
  43.7 1.0 %copy-start.3 = (f32[4,4,1024]{2,1,0:T(4,128)S(1)}, f32[4,4,1024]{2,1,0:T(4,128)}, u32[]{:S(2)}) copy-start(f32[4,4,1024]{2,1,0:T(4,128)} %get-tuple-element.19) | copy-start | bytes 196612
  43.7 1.0 %copy-start.4 = (f32[4,4,1024]{2,1,0:T(4,128)S(1)}, f32[4,4,1024]{2,1,0:T(4,128)}, u32[]{:S(2)}) copy-start(f32[4,4,1024]{2,1,0:T(4,128)} %get-tuple-element.20) | copy-start | bytes 196612
  43.7 1.0 %copy-start.7 = (f32[4,16,4]{2,1,0:T(8,128)S(1)}, f32[4,16,4]{2,1,0:T(8,128)}, u32[]{:S(2)}) copy-start(f32[4,16,4]{2,1,0:T(8,128)} %copy-done.6) | copy-start | bytes 3076
  43.7 1.0 %copy-start.8 = (f32[4,2,1024]{2,1,0:T(2,128)S(1)}, f32[4,2,1024]{2,1,0:T(2,128)}, u32[]{:S(2)}) copy-start(f32[4,2,1024]{2,1,0:T(2,128)} %get-tuple-element.11) | copy-start | bytes 98308
  43.7 1.0 %copy-start.9 = (f32[4,2,1024]{2,1,0:T(2,128)S(1)}, f32[4,2,1024]{2,1,0:T(2,128)}, u32[]{:S(2)}) copy-start(f32[4,2,1024]{2,1,0:T(2,128)} %get-tuple-element.12) | copy-start | bytes 98308
  43.8 1.0 %copy-start.11 = (f32[4,1,1024]{2,1,0:T(1,128)S(1)}, f32[4,1,1024]{2,1,0:T(1,128)}, u32[]{:S(2)}) copy-start(f32[4,1,1024]{2,1,0:T(1,128)} %get-tuple-element.8) | copy-start | bytes 49156
  43.8 1.0 %copy-start.14 = (pred[4]{0:T(512)(128)(4,1)S(1)}, pred[4]{0:T(512)(128)(4,1)}, u32[]{:S(2)}) copy-start(pred[4]{0:T(512)(128)(4,1)} %iota_compare_fusion.1) | copy-start | bytes 16
  46.0 0.7 copy-start.5
Sparse Core Ops, SparseCore 0:
  56.3 8.8 reduce-scatter.1
where the time goes:
time: 88.1 us; the launch traced here: 87.6 us
  matrix products  18 us (20%)
  blocking collectives  16 us (18%)
  between operations  15 us (17%)
  starting transfers between devices  14.4 us (16%)
  local copies, waits for them, and re-layouts  10.9 us (12%)
  waiting for transfers between devices  9.81 us (11%)
  other arithmetic  3.57 us (4%)
    all_to_all x1, blocking collectives, per_device(): lax.all_to_all(summed, ('row', 'col'), split_axis=1, concat_axis=0, tiled...  14 us
    dot_general x1, matrix products, per_device(): lax.dot_general(coarse_density.reshape(-1, half_cells), table, (((1,), (1...  9.47 us
    reduce_scatter x1, waiting for transfers between devices, per_device(): lax.psum_scatter(partial_value, 'grp', scatter_dimension=2, tiled=True)  8.98 us
    dot_general x1, matrix products, per_device(): jnp.dot(shard_piece.reshape(-1, count_here), table, preferred_element_typ...  8.56 us
    all_to_all x1, starting transfers between devices, per_device(): lax.all_to_all(velocity, ('row', 'col'), split_axis=1, concat_axis=2, til...  8.34 us
    ppermute x2, starting transfers between devices, with_halo(): lax.ppermute(lax.slice_in_dim(block, 0, width, axis=dim), axis, backward)  5.98 us
    unnamed x34, local copies, waits for them, and re-layouts  3.62 us
    slice x8, local copies, waits for them, and re-layouts, tendency(): ahead = jnp.roll(field, -reach, axis=1)  2.77 us
  transfers between devices with their start and end apart: 6, of which 2 were waited for; matrix products, arithmetic and copies ran while one was open for 20% of the time, Pallas kernels for 0%

commit v1 on v0

v1 whole, which is shorter than its diff:
```python
import functools
import math

import jax
import jax.numpy as jnp
import numpy as np
from jax import lax
from jax.experimental import pallas as pl
from jax.experimental.pallas import tpu as pltpu
from jax.sharding import PartitionSpec as P

first_coef = (4.0 / 5.0, -1.0 / 5.0, 4.0 / 105.0, -1.0 / 280.0)
second_coef = (8.0 / 5.0, -1.0 / 5.0, 8.0 / 315.0, -1.0 / 560.0)
centre_coef = -205.0 / 72.0
kappa_value = 0.1
step_value = 0.2
strat_value = 1.0

LANES = 128
GROUP = 16
ALL = ("grp", "row", "col")


def half_table(mode_count, fine_cells):
    k = np.arange(mode_count)
    half = mode_count // 2
    frequency = np.where(k < half, k, k - half + 1)
    phase = frequency[:, None] * np.arange(fine_cells // 2)[None, :] % fine_cells
    angle = phase.astype(np.float32) * np.float32(2.0 * math.pi / fine_cells)
    table = np.where((k < half)[:, None], np.cos(angle), np.sin(angle)).astype(np.float32)
    order = k.reshape(2, half // LANES, LANES).transpose(1, 0, 2).reshape(-1)
    sign = np.where(frequency % 2 == 0, 1.0, -1.0)
    return table[order].astype(jnp.bfloat16), sign[order].astype(np.float32)[None, :]


def selector(out_axes, in_axes, sizes):
    count = math.prod(sizes[a] for a in in_axes)
    index = np.arange(count).reshape([sizes[a] for a in in_axes])
    source = index.transpose([in_axes.index(a) for a in out_axes]).reshape(-1)
    matrix = np.zeros((count, count), np.float32)
    matrix[np.arange(count), source] = 1.0
    return matrix.astype(jnp.bfloat16)


def exact(matrix, rows):
    return jnp.dot(matrix, rows, preferred_element_type=jnp.float32).astype(jnp.bfloat16)


def prepare_kernel(planes, vel_ref, dens_ref, mat_ref, send_ref, dens16_ref, edge_ref):
    comps, depth, modes = vel_ref.shape
    tiles = modes // LANES
    step = GROUP * planes
    chunk = comps * planes * tiles * GROUP
    for b in range(depth // step):
        parts = []
        for c in range(comps):
            rows = vel_ref[c, pl.ds(b * step, step), :]
            for h in range(tiles):
                parts.append(rows[:, h * LANES : (h + 1) * LANES])
        mixed = exact(mat_ref[...], jnp.concatenate(parts, axis=0))
        send_ref[0, pl.ds(b * chunk, chunk), :] = mixed
        send_ref[1, pl.ds(b * chunk, chunk), :] = mixed
    cells = dens_ref.shape[2]
    for p in range(planes):
        field = dens_ref[p]
        dens16_ref[p] = field.astype(jnp.bfloat16)
        lane = lax.broadcasted_iota(jnp.int32, (field.shape[0], LANES), 1)
        edge_ref[p] = jnp.where(lane < LANES // 2, field[:, :LANES], field[:, cells - LANES :])


def stencil_kernel(dens_ref, low_ref, high_ref, edge_ref, gx_ref, gy_ref, gz_ref, base_ref, zz_ref):
    planes, rows, cells = dens_ref.shape
    zz_ref[pl.ds(0, planes)] = low_ref[...].astype(jnp.float32)
    zz_ref[pl.ds(planes, planes)] = dens_ref[...]
    zz_ref[pl.ds(2 * planes, planes)] = high_ref[...].astype(jnp.float32)

    def one(p):
        field = dens_ref[p]
        wide = jnp.concatenate([field, edge_ref[p]], axis=1)
        span = wide.shape[1]
        grad_x = grad_y = grad_z = lap = None
        for reach in range(1, 5):
            ahead_x = pltpu.roll(wide, span - reach, 1)[:, :cells]
            behind_x = pltpu.roll(wide, reach, 1)[:, :cells]
            ahead_y = pltpu.roll(field, rows - reach, 0)
            behind_y = pltpu.roll(field, reach, 0)
            ahead_z = zz_ref[p + planes + reach]
            behind_z = zz_ref[p + planes - reach]
            a = step_value * first_coef[reach - 1]
            b = step_value * kappa_value * second_coef[reach - 1]
            total = (ahead_x + behind_x) + (ahead_y + behind_y) + (ahead_z + behind_z)
            if reach == 1:
                grad_x = a * (ahead_x - behind_x)
                grad_y = a * (ahead_y - behind_y)
                grad_z = a * (ahead_z - behind_z) + step_value * strat_value
                lap = (1.0 + step_value * kappa_value * 3.0 * centre_coef) * field + b * total
            else:
                grad_x = grad_x + a * (ahead_x - behind_x)
                grad_y = grad_y + a * (ahead_y - behind_y)
                grad_z = grad_z + a * (ahead_z - behind_z)
                lap = lap + b * total
        gx_ref[p] = grad_x
        gy_ref[p] = grad_y
        gz_ref[p] = grad_z
        base_ref[p] = lap

    loop_planes(planes, rows, one)


def loop_planes(planes, rows, body):
    if rows <= GROUP:
        for p in range(planes):
            body(p)
    else:
        lax.fori_loop(0, planes, lambda p, _: (body(p), 0)[1], 0)


def advance_kernel(
    scale, live_ref, side_ref, recv_ref, table_ref, sign_ref, in_mat_ref, out_mat_ref,
    dens_ref, gx_ref, gy_ref, gz_ref, base_ref, next_ref, send_ref, fine_ref,
):
    planes, rows, cells = dens_ref.shape
    modes = table_ref.shape[0]
    tiles = modes // (2 * LANES)
    comps = 3
    chunk = comps * planes * tiles * GROUP
    per_tile = chunk // tiles
    sign = jnp.where(side_ref[0] == 0, jnp.ones_like(sign_ref[...]), sign_ref[...])
    back = GROUP * planes * tiles
    for b in range(rows // GROUP):
        lanes = [recv_ref[g, pl.ds(b * chunk, chunk), :] for g in range(2)]
        mixed = jnp.dot(
            in_mat_ref[...], jnp.concatenate(lanes, axis=1), preferred_element_type=jnp.float32
        )
        coarse = jnp.concatenate(
            [mixed[h * per_tile : (h + 1) * per_tile] for h in range(tiles)], axis=1
        )
        coarse = (coarse * sign).astype(jnp.bfloat16)
        fine_ref[...] = jnp.dot(coarse, table_ref[...], preferred_element_type=jnp.float32)
        here = pl.ds(b * GROUP, GROUP)
        parts = []
        for p in range(planes):
            vel = [fine_ref[pl.ds((c * planes + p) * GROUP, GROUP), :] for c in range(comps)]
            moved = base_ref[p, here, :] - (
                vel[0] * gx_ref[p, here, :] + vel[1] * gy_ref[p, here, :] + vel[2] * gz_ref[p, here, :]
            )
            value = jnp.where(p < live_ref[0], moved, dens_ref[p, here, :])
            next_ref[p, here, :] = value
            parts.append(value.astype(jnp.bfloat16))
        lifted = lax.dot_general(
            jnp.concatenate(parts, axis=0), table_ref[...], (((1,), (1,)), ((), ())),
            preferred_element_type=jnp.float32,
        )
        lifted = (lifted * (sign * scale)).astype(jnp.bfloat16)
        stacked = jnp.concatenate(
            [lifted[:, h * 2 * LANES : (h + 1) * 2 * LANES] for h in range(tiles)], axis=0
        )
        ordered = exact(out_mat_ref[...], stacked)
        for g in range(2):
            send_ref[g, pl.ds(b * back, back), :] = ordered[:, g * LANES : (g + 1) * LANES]


def per_device(velocity, density, live_planes):
    comps, depth, _, modes = velocity.shape
    planes, rows, cells = density.shape
    slabs = depth // planes
    tiles = modes // LANES
    fine_cells = 2 * cells
    table, sign = half_table(2 * modes, fine_cells)
    sizes = dict(s=GROUP, c=comps, p=planes, h=tiles, y=GROUP)
    prep_mat = selector("shcp", "chsp", sizes)
    in_mat = selector("hcpy", "yhcp", sizes)
    out_mat = selector("yph", "hpy", sizes)
    chunk = comps * planes * tiles
    vmem = pl.BlockSpec(memory_space=pltpu.VMEM)
    smem = pl.BlockSpec(memory_space=pltpu.SMEM)
    params = pltpu.CompilerParams(vmem_limit_bytes=(24 if rows <= GROUP else 56) * 2**20)
    f32, b16 = jnp.float32, jnp.bfloat16

    send, dens16, edge = pl.pallas_call(
        functools.partial(prepare_kernel, planes),
        out_shape=(
            jax.ShapeDtypeStruct((2, slabs * chunk, LANES), b16),
            jax.ShapeDtypeStruct(density.shape, b16),
            jax.ShapeDtypeStruct((planes, rows, LANES), f32),
        ),
        in_specs=[vmem] * 3,
        out_specs=(vmem,) * 3,
        compiler_params=params,
        name="prepare",
    )(velocity.reshape(comps, depth, modes), density, prep_mat)

    count = slabs
    forward = [(i, (i + 1) % count) for i in range(count)]
    backward = [(target, source) for source, target in forward]
    other = lax.ppermute(edge, "grp", [(0, 1), (1, 0)])
    low = lax.ppermute(dens16, ("row", "col"), forward)
    high = lax.ppermute(dens16, ("row", "col"), backward)
    recv = lax.all_to_all(send.reshape(2 * slabs, chunk, LANES), ALL, 0, 0, tiled=True)
    recv = recv.reshape(2, slabs * chunk, LANES)

    field = jax.ShapeDtypeStruct(density.shape, f32)
    grads = pl.pallas_call(
        stencil_kernel,
        out_shape=(field,) * 4,
        in_specs=[vmem] * 4,
        out_specs=(vmem,) * 4,
        scratch_shapes=[pltpu.VMEM((3 * planes, rows, cells), f32)],
        compiler_params=params,
        cost_estimate=pl.CostEstimate(flops=60 * density.size, bytes_accessed=24 * density.size, transcendentals=0),
        name="stencil",
    )(density, low, high, other)

    side = lax.axis_index("grp").reshape(1)
    scale = -math.sqrt(2.0 / fine_cells)
    density_next, back = pl.pallas_call(
        functools.partial(advance_kernel, scale),
        out_shape=(field, jax.ShapeDtypeStruct((2, rows * planes * tiles, LANES), b16)),
        in_specs=[smem, smem] + [vmem] * 10,
        out_specs=(vmem,) * 2,
        scratch_shapes=[pltpu.VMEM((comps * planes * GROUP, cells), f32)],
        compiler_params=params,
        name="advance",
    )(live_planes, side, recv, table, sign, in_mat, out_mat, density, *grads)

    home = lax.all_to_all(back.reshape(2 * rows, planes * tiles, LANES), ALL, 0, 0, tiled=True)
    home = home.reshape(2, slabs * planes * tiles, LANES).astype(f32)
    buoyancy = (home[0] + home[1]).reshape(depth, 1, modes)
    return (density_next, buoyancy)


def solution(mesh):
    in_specs = (
        P(None, None, ("row", "col"), "grp"),
        P(("row", "col"), None, "grp"),
        P(("row", "col")),
    )
    out_specs = (P(("row", "col"), None, "grp"), P(None, ("row", "col"), "grp"))
    return jax.shard_map(
        per_device, mesh=mesh, in_specs=in_specs, out_specs=out_specs, check_vma=False
    )
```

time: 88.1 us -> 41.3 us (0.47)
  matrix products: 18 us -> 0 us
  between operations: 15 us -> 1.36 us
  blocking collectives: 16 us -> 9 us
  local copies, waits for them, and re-layouts: 10.9 us -> 4.69 us
  Pallas kernels: 0 us -> 3.19 us
  other arithmetic: 3.57 us -> 0.65 us
  starting transfers between devices: 14.4 us -> 12.8 us
    dot_general x2 -> x0, matrix products: 18 us -> none  [the longest x1 9.47 us: per_device(): lax.dot_general(coarse_density.reshape(-1, half_cells), table, (((1,), (1...]
    reduce_scatter x1 -> x0, waiting for transfers between devices: 8.98 us -> none  [per_device(): lax.psum_scatter(partial_value, 'grp', scatter_dimension=2, tiled=True)]
    ppermute x4 -> x3, waiting for transfers between devices: 0.82 us -> 9.23 us  [the longest x1 5.99 us: per_device(): low = lax.ppermute(dens16, ('row', 'col'), forward)]
    all_to_all x1, blocking collectives: 14 us -> 9 us  [per_device(): lax.all_to_all(back.reshape(2 * rows, planes * tiles, LANES), ALL, 0, 0,...]
    slice x10 -> x0, local copies, waits for them, and re-layouts: 3.72 us -> none  [the longest x8 2.77 us: tendency(): ahead = jnp.roll(field, -reach, axis=1)]
    pallas_call x0 -> x3, Pallas kernels: none -> 3.19 us  [the longest x1 1.46 us: per_device(): pl.pallas_call(functools.partial(advance_kernel, scale), out_shape=(field...]
    all_gather x1 -> x0, blocking collectives: 1.95 us -> none  [per_device(): shard_piece = lax.all_gather(received, 'grp', axis=3, tiled=True)]
    select_n x2 -> x0, other arithmetic: 1.85 us -> none  [the longest x1 1.26 us: per_device(): density_next = jnp.where(active, density + step_value * change, density)]
  transfers between devices with their start and end apart: 6 -> 4, of which waited for: 2 -> 3; matrix products, arithmetic and copies ran while one was open for 20% -> 0% of each run, Pallas kernels for 0% -> 2%
where the time goes in v1:
time: 41.3 us; the launch traced here: 41 us
  starting transfers between devices  12.8 us (31%)
  waiting for transfers between devices  9.23 us (22%)
  blocking collectives  9 us (22%)
  local copies, waits for them, and re-layouts  4.69 us (11%)
  Pallas kernels  3.19 us (8%)
  between operations  1.36 us (3%)
  other arithmetic  0.65 us (2%)
    all_to_all x1, blocking collectives, per_device(): lax.all_to_all(back.reshape(2 * rows, planes * tiles, LANES), ALL, 0, 0,...  9 us
    all_to_all x1, starting transfers between devices, per_device(): lax.all_to_all(send.reshape(2 * slabs, chunk, LANES), ALL, 0, 0, tiled=True)  7.3 us
    ppermute x1, waiting for transfers between devices, per_device(): low = lax.ppermute(dens16, ('row', 'col'), forward)  5.99 us
    ppermute x1, starting transfers between devices, per_device(): high = lax.ppermute(dens16, ('row', 'col'), backward)  5.52 us
    unnamed x16, local copies, waits for them, and re-layouts  4.69 us
    ppermute x1, waiting for transfers between devices, per_device(): high = lax.ppermute(dens16, ('row', 'col'), backward)  2.69 us
    pallas_call x1, Pallas kernels, per_device(): pl.pallas_call(functools.partial(advance_kernel, scale), out_shape=(field...  1.46 us
    pallas_call x1, Pallas kernels, per_device(): pl.pallas_call(functools.partial(prepare_kernel, planes), out_shape=(jax....  0.92 us
  transfers between devices with their start and end apart: 4, of which 3 were waited for; matrix products, arithmetic and copies ran while one was open for 0% of the time, Pallas kernels for 2%

profile of v1, /device:TPU:0, one launch (start us, length us, event | category | flops | bytes accessed | tf_op | source)
XLA Modules:
  0.0 41.0 jit_solution(4638967124152146762)
XLA Ops:
  0.6 0.0 copy-start
  0.6 0.9 %copy-done = f32[4,16,1024]{2,1,0:T(8,128)S(1)} copy-done((f32[4,16,1024]{2,1,0:T(8,128)S(1)}, f32[4,16,1024]{2,1,0:T(8,128)}, u32[]{:S(2)}) %copy-start) | copy-done | bytes 262168
  1.6 0.0 copy-start.4
  1.6 1.0 %copy-done.4 = bf16[384,384]{1,0:T(8,128)(2,1)S(1)} copy-done((bf16[384,384]{1,0:T(8,128)(2,1)S(1)}, bf16[384,384]{1,0:T(8,128)(2,1)}, u32[]{:S(2)}) %copy-start.4) | copy-done | bytes 294936
  2.5 0.0 copy-start.5
  2.5 0.9 %copy-done.5 = bf16[3,64,1,256]{3,1,2,0:T(8,128)(2,1)S(1)} copy-done((bf16[3,64,1,256]{3,1,2,0:T(8,128)(2,1)S(1)}, bf16[3,64,1,256]{3,1,2,0:T(8,128)(2,1)}, u32[]{:S(2)}) %copy-start.5) | copy-done | bytes 98328
  3.4 0.9 %prepare.1 = (bf16[2,384,128]{2,1,0:T(8,128)(2,1)}, bf16[4,16,1024]{2,1,0:T(8,128)(2,1)S(1)}, f32[4,16,128]{2,1,0:T(8,128)S(1)}) custom-call(bf16[3,64,256]{2,1,0:T(8,128)(2,1)S(1)} %bitcast.7, f32[4,16,1024]{2,1,0:T(8,128)S(1)} %copy-done, bf16[384,384]{1,0:T(8,128)(2,1)S(1)} %copy-done.4), custom_call_target="tpu_custom_call" | custom-call | tf_op jit(solution)/shard_map/prepare/pallas_call | solution.py:180
  4.4 0.0 copy-start.1
  4.4 7.3 %all-to-all-start = ((bf16[32,24,128]{2,1,0:T(8,128)(2,1)}), bf16[32,24,128]{2,1,0:T(8,128)(2,1)S(1)}, u32[]{:S(2)}, u32[]{:S(2)}) async-start(bf16[32,24,128]{2,1,0:T(8,128)(2,1)} %bitcast.2), calls=%async_computation | async-start | bytes 393216 | tf_op jit(solution)/shard_map/all_to_all | solution.py:199
  11.7 0.0 copy-start.3
  11.7 5.5 %collective-permute-start.1 = (bf16[4,16,1024]{2,1,0:T(8,128)(2,1)S(1)}, bf16[4,16,1024]{2,1,0:T(8,128)(2,1)S(1)}, u32[]{:S(2)}, u32[]{:S(2)}) collective-permute-start(bf16[4,16,1024]{2,1,0:T(8,128)(2,1)S(1)} %get-tuple-element.12), channel_id=1, source_target_pairs={{1,0},{2,1},{3,2},{4,3},{5,4},{6,5},{7,6},{8,7},{9,8},{10,9},{11,1... | collective-permute-start | bytes 393224 | tf_op jit(solution)/shard_map/ppermute | solution.py:198
  17.2 0.0 collective-permute-start
  17.2 0.0 collective-permute-start.2
  17.9 0.6 %collective-permute-done.2.edge_ref = f32[4,16,128]{2,1,0:T(8,128)S(1)} collective-permute-done((f32[4,16,128]{2,1,0:T(8,128)S(1)}, f32[4,16,128]{2,1,0:T(8,128)S(1)}, u32[]{:S(2)}, u32[]{:S(2)}) %collective-permute-start.2) | collective-permute-done | bytes 32800 | tf_op jit(solution)/shard_map/ppermute | solution.py:196
  18.4 2.7 %collective-permute-done.1.high_ref = bf16[4,16,1024]{2,1,0:T(8,128)(2,1)S(1)} collective-permute-done((bf16[4,16,1024]{2,1,0:T(8,128)(2,1)S(1)}, bf16[4,16,1024]{2,1,0:T(8,128)(2,1)S(1)}, u32[]{:S(2)}, u32[]{:S(2)}) %collective-permute-start.1) | collective-permute-done | bytes 131104 | tf_op jit(solution)/shard_map/ppermute | solution.py:198
  21.1 6.0 %collective-permute-done.low_ref = bf16[4,16,1024]{2,1,0:T(8,128)(2,1)S(1)} collective-permute-done((bf16[4,16,1024]{2,1,0:T(8,128)(2,1)S(1)}, bf16[4,16,1024]{2,1,0:T(8,128)(2,1)S(1)}, u32[]{:S(2)}, u32[]{:S(2)}) %collective-permute-start) | collective-permute-done | bytes 131104 | tf_op jit(solution)/shard_map/ppermute | solution.py:197
  27.1 0.0 copy-done.1
  27.1 0.0 copy-start.6
  27.1 0.8 %stencil.1 = (f32[4,16,1024]{2,1,0:T(8,128)S(1)}, f32[4,16,1024]{2,1,0:T(8,128)S(1)}, f32[4,16,1024]{2,1,0:T(8,128)S(1)}, f32[4,16,1024]{2,1,0:T(8,128)S(1)}) custom-call(f32[4,16,1024]{2,1,0:T(8,128)S(1)} %copy-done.1, bf16[4,16,1024]{2,1,0:T(8,128)(2,1)S(1)} %collective-permute-done.low_ref, bf16[4,16,1024]{2,1,0:T(8,128)(2,1)S(1)} %collective-permute-done.1.high_ref, ...), custom_call_target="tpu_custom_call" | custom-call | flops 3932160 | bytes 1572864 | tf_op jit(solution)/shard_map/stencil/pallas_call | solution.py:203
  27.9 0.0 all-to-all-done
  27.9 0.0 copy-start.7
  27.9 0.0 copy-done.3
  28.0 0.0 copy-done.6
  28.0 0.7 %copy-done.7 = f32[1,512]{1,0:T(1,128)S(1)} copy-done((f32[1,512]{1,0:T(1,128)S(1)}, f32[1,512]{1,0:T(1,128)}, u32[]{:S(2)}) %copy-start.7) | copy-done | bytes 2072
  28.6 0.0 copy-start.2
  28.6 1.2 %copy-done.2 = bf16[512,1024]{1,0:T(8,128)(2,1)S(1)} copy-done((bf16[512,1024]{1,0:T(8,128)(2,1)S(1)}, bf16[512,1024]{1,0:T(8,128)(2,1)}, u32[]{:S(2)}) %copy-start.2) | copy-done | bytes 1048600
  29.8 1.5 %advance.1 = (f32[4,16,1024]{2,1,0:T(8,128)}, bf16[2,128,128]{2,1,0:T(8,128)(2,1)S(1)}) custom-call(s32[1]{0:T(128)S(6)} %copy.10.live_ref, s32[1]{0:T(128)} %bitcast.side_ref, bf16[2,384,128]{2,1,0:T(8,128)(2,1)S(1)} %bitcast.6, bf16[512,1024]{1,0:T(8,128)(2,1)S(1)} %copy-done.2, f32[1,512]{1,0:T(1,128)S(1)} %copy-done.7, bf16[384,384]{1,0:T(8,128)(2,1)S(1)} %copy-done.3, ...), custom_call_target="tpu_custom_call" | custom-call | tf_op jit(solution)/shard_map/advance/pallas_call | solution.py:216
  31.3 9.0 %all_to_all.10 = bf16[32,8,128]{2,1,0:T(8,128)(2,1)S(1)} all-to-all(bf16[32,8,128]{2,1,0:T(8,128)(2,1)S(1)} %bitcast.8), channel_id=1, replica_groups=mesh['grp'=2,'row'=4,'col'=4] {'grp','row','col'}, dimensions={0} | all-to-all | bytes 131072 | tf_op jit(solution)/shard_map/all_to_all | solution.py:226
  40.3 0.6 %slice_add_fusion = f32[16,8,128]{2,1,0:T(8,128)} fusion(f32[32,8,128]{2,1,0:T(8,128)S(1)} %convert_element_type.4), kind=kLoop, calls=%fused_computation | loop fusion | flops 16384 | bytes 196608 | tf_op jit(solution)/shard_map/add | solution.py:228
  (1 shorter events, 0.0 us)
Async XLA Ops:
  0.6 1.0 %copy-start = (f32[4,16,1024]{2,1,0:T(8,128)S(1)}, f32[4,16,1024]{2,1,0:T(8,128)}, u32[]{:S(2)}) copy-start(f32[4,16,1024]{2,1,0:T(8,128)} %dens_ref.5) | copy-start | bytes 786436
  1.6 1.0 %copy-start.4 = (bf16[384,384]{1,0:T(8,128)(2,1)S(1)}, bf16[384,384]{1,0:T(8,128)(2,1)}, u32[]{:S(2)}) copy-start(bf16[384,384]{1,0:T(8,128)(2,1)} %constant.16.clone.mat_ref) | copy-start | bytes 884740
  2.5 0.9 %copy-start.5 = (bf16[3,64,1,256]{3,1,2,0:T(8,128)(2,1)S(1)}, bf16[3,64,1,256]{3,1,2,0:T(8,128)(2,1)}, u32[]{:S(2)}) copy-start(bf16[3,64,1,256]{3,1,2,0:T(8,128)(2,1)} %param.8) | copy-start | bytes 294916
  4.4 22.7 %copy-start.1 = (f32[4,16,1024]{2,1,0:T(8,128)S(1)}, f32[4,16,1024]{2,1,0:T(8,128)}, u32[]{:S(2)}) copy-start(f32[4,16,1024]{2,1,0:T(8,128)} %dens_ref.5) | copy-start | bytes 786436
  4.4 23.6 %all-to-all-start = ((bf16[32,24,128]{2,1,0:T(8,128)(2,1)}), bf16[32,24,128]{2,1,0:T(8,128)(2,1)S(1)}, u32[]{:S(2)}, u32[]{:S(2)}) async-start(bf16[32,24,128]{2,1,0:T(8,128)(2,1)} %bitcast.2), calls=%async_computation | async-start | bytes 393216 | tf_op jit(solution)/shard_map/all_to_all | solution.py:199
  11.7 16.3 %copy-start.3 = (bf16[384,384]{1,0:T(8,128)(2,1)S(1)}, bf16[384,384]{1,0:T(8,128)(2,1)}, u32[]{:S(2)}) copy-start(bf16[384,384]{1,0:T(8,128)(2,1)} %constant.19.clone.in_mat_ref) | copy-start | bytes 884740
  11.7 9.4 %collective-permute-start.1 = (bf16[4,16,1024]{2,1,0:T(8,128)(2,1)S(1)}, bf16[4,16,1024]{2,1,0:T(8,128)(2,1)S(1)}, u32[]{:S(2)}, u32[]{:S(2)}) collective-permute-start(bf16[4,16,1024]{2,1,0:T(8,128)(2,1)S(1)} %get-tuple-element.12), channel_id=1, source_target_pairs={{1,0},{2,1},{3,2},{4,3},{5,4},{6,5},{7,6},{8,7},{9,8},{10,9},{11,1... | collective-permute-start | bytes 393224 | tf_op jit(solution)/shard_map/ppermute | solution.py:198
  17.2 9.9 %collective-permute-start = (bf16[4,16,1024]{2,1,0:T(8,128)(2,1)S(1)}, bf16[4,16,1024]{2,1,0:T(8,128)(2,1)S(1)}, u32[]{:S(2)}, u32[]{:S(2)}) collective-permute-start(bf16[4,16,1024]{2,1,0:T(8,128)(2,1)S(1)} %get-tuple-element.12), channel_id=1, source_target_pairs={{0,1},{1,2},{2,3},{3,4},{4,5},{5,6},{6,7},{7,8},{8,9},{9,10},{10,1... | collective-permute-start | bytes 393224 | tf_op jit(solution)/shard_map/ppermute | solution.py:197
  17.2 1.2 %collective-permute-start.2 = (f32[4,16,128]{2,1,0:T(8,128)S(1)}, f32[4,16,128]{2,1,0:T(8,128)S(1)}, u32[]{:S(2)}, u32[]{:S(2)}) collective-permute-start(f32[4,16,128]{2,1,0:T(8,128)S(1)} %get-tuple-element.13), channel_id=1, source_target_pairs={{0,16},{16,0},{1,17},{17,1},{2,18},{18,2},{3,19},{19,3},{4,20},{20... | collective-permute-start | bytes 98312 | tf_op jit(solution)/shard_map/ppermute | solution.py:196
  27.1 0.9 %copy-start.6 = (bf16[128,128]{1,0:T(8,128)(2,1)S(1)}, bf16[128,128]{1,0:T(8,128)(2,1)}, u32[]{:S(2)}) copy-start(bf16[128,128]{1,0:T(8,128)(2,1)} %constant.20.clone.out_mat_ref) | copy-start | bytes 98308
  27.9 0.7 %copy-start.7 = (f32[1,512]{1,0:T(1,128)S(1)}, f32[1,512]{1,0:T(1,128)}, u32[]{:S(2)}) copy-start(f32[1,512]{1,0:T(1,128)} %constant.18.clone.sign_ref) | copy-start | bytes 6148
  28.6 1.2 %copy-start.2 = (bf16[512,1024]{1,0:T(8,128)(2,1)S(1)}, bf16[512,1024]{1,0:T(8,128)(2,1)}, u32[]{:S(2)}) copy-start(bf16[512,1024]{1,0:T(8,128)(2,1)} %constant.17.clone.table_ref) | copy-start | bytes 3145732

commit v2 on v1

--- a/solution.py
+++ b/solution.py
@@ -19,18 +19,19 @@
 LANES = 128
 GROUP = 16
 ALL = ("grp", "row", "col")
-
-
-def half_table(mode_count, fine_cells):
+STENCIL_FLOPS = 2 * 10**10
+
+
+def half_tables(mode_count, fine_cells):
     k = np.arange(mode_count)
     half = mode_count // 2
     frequency = np.where(k < half, k, k - half + 1)
-    phase = frequency[:, None] * np.arange(fine_cells // 2)[None, :] % fine_cells
+    phase = frequency[:, None] * np.arange(fine_cells)[None, :] % fine_cells
     angle = phase.astype(np.float32) * np.float32(2.0 * math.pi / fine_cells)
     table = np.where((k < half)[:, None], np.cos(angle), np.sin(angle)).astype(np.float32)
     order = k.reshape(2, half // LANES, LANES).transpose(1, 0, 2).reshape(-1)
-    sign = np.where(frequency % 2 == 0, 1.0, -1.0)
-    return table[order].astype(jnp.bfloat16), sign[order].astype(np.float32)[None, :]
+    table = table[order].reshape(mode_count, 2, fine_cells // 2).transpose(1, 0, 2)
+    return np.ascontiguousarray(table).astype(jnp.bfloat16)
 
 
 def selector(out_axes, in_axes, sizes):
@@ -46,11 +47,31 @@
     return jnp.dot(matrix, rows, preferred_element_type=jnp.float32).astype(jnp.bfloat16)
 
 
-def prepare_kernel(planes, vel_ref, dens_ref, mat_ref, send_ref, dens16_ref, edge_ref):
+def prepare_kernel(
+    planes, vel_hbm, dens_hbm, mat_hbm, send_ref, dens16_ref, edge_ref,
+    vel_ref, dens_ref, mat_ref, sems,
+):
+    copies = [
+        pltpu.make_async_copy(source, target, sems.at[i])
+        for i, (source, target) in enumerate(
+            [(dens_hbm, dens_ref), (vel_hbm, vel_ref), (mat_hbm, mat_ref)]
+        )
+    ]
+    for copy in copies:
+        copy.start()
     comps, depth, modes = vel_ref.shape
     tiles = modes // LANES
     step = GROUP * planes
     chunk = comps * planes * tiles * GROUP
+    cells = dens_ref.shape[2]
+    copies[0].wait()
+    for p in range(planes):
+        field = dens_ref[p]
+        dens16_ref[p] = field.astype(jnp.bfloat16)
+        lane = lax.broadcasted_iota(jnp.int32, (field.shape[0], LANES), 1)
+        edge_ref[p] = jnp.where(lane < LANES // 2, field[:, :LANES], field[:, cells - LANES :])
+    copies[1].wait()
+    copies[2].wait()
     for b in range(depth // step):
         parts = []
         for c in range(comps):
@@ -60,22 +81,31 @@
         mixed = exact(mat_ref[...], jnp.concatenate(parts, axis=0))
         send_ref[0, pl.ds(b * chunk, chunk), :] = mixed
         send_ref[1, pl.ds(b * chunk, chunk), :] = mixed
-    cells = dens_ref.shape[2]
-    for p in range(planes):
-        field = dens_ref[p]
-        dens16_ref[p] = field.astype(jnp.bfloat16)
-        lane = lax.broadcasted_iota(jnp.int32, (field.shape[0], LANES), 1)
-        edge_ref[p] = jnp.where(lane < LANES // 2, field[:, :LANES], field[:, cells - LANES :])
-
-
-def stencil_kernel(dens_ref, low_ref, high_ref, edge_ref, gx_ref, gy_ref, gz_ref, base_ref, zz_ref):
-    planes, rows, cells = dens_ref.shape
+
+
+def stencil_kernel(
+    side_ref, dens_hbm, low_ref, high_ref, edge_ref, table_hbm, in_hbm, out_hbm,
+    gx_ref, gy_ref, gz_ref, base_ref, field_ref, table_ref, in_ref, out_ref, zz_ref, sems,
+):
+    planes, rows, cells = dens_hbm.shape
+    copies = [
+        pltpu.make_async_copy(source, target, sems.at[i])
+        for i, (source, target) in enumerate(
+            [
+                (dens_hbm, field_ref), (table_hbm.at[side_ref[0]], table_ref),
+                (in_hbm, in_ref), (out_hbm, out_ref),
+            ]
+        )
+    ]
+    for copy in copies:
+        copy.start()
     zz_ref[pl.ds(0, planes)] = low_ref[...].astype(jnp.float32)
-    zz_ref[pl.ds(planes, planes)] = dens_ref[...]
     zz_ref[pl.ds(2 * planes, planes)] = high_ref[...].astype(jnp.float32)
+    copies[0].wait()
+    zz_ref[pl.ds(planes, planes)] = field_ref[...]
 
     def one(p):
-        field = dens_ref[p]
+        field = field_ref[p]
         wide = jnp.concatenate([field, edge_ref[p]], axis=1)
         span = wide.shape[1]
         grad_x = grad_y = grad_z = lap = None
@@ -105,6 +135,8 @@
         base_ref[p] = lap
 
     loop_planes(planes, rows, one)
+    for copy in copies[1:]:
+        copy.wait()
 
 
 def loop_planes(planes, rows, body):
@@ -116,8 +148,8 @@
 
 
 def advance_kernel(
-    scale, live_ref, side_ref, recv_ref, table_ref, sign_ref, in_mat_ref, out_mat_ref,
-    dens_ref, gx_ref, gy_ref, gz_ref, base_ref, next_ref, send_ref, fine_ref,
+    scale, live_ref, recv_ref, table_ref, in_mat_ref, out_mat_ref,
+    dens_ref, gx_ref, gy_ref, gz_ref, base_ref, next_hbm, send_ref, fine_ref, next_ref, sems,
 ):
     planes, rows, cells = dens_ref.shape
     modes = table_ref.shape[0]
@@ -125,17 +157,17 @@
     comps = 3
     chunk = comps * planes * tiles * GROUP
     per_tile = chunk // tiles
-    sign = jnp.where(side_ref[0] == 0, jnp.ones_like(sign_ref[...]), sign_ref[...])
     back = GROUP * planes * tiles
-    for b in range(rows // GROUP):
+    groups = rows // GROUP
+    copies = [
+        pltpu.make_async_copy(next_ref.at[p], next_hbm.at[p], sems.at[p]) for p in range(planes)
+    ]
+    for b in range(groups):
         lanes = [recv_ref[g, pl.ds(b * chunk, chunk), :] for g in range(2)]
-        mixed = jnp.dot(
-            in_mat_ref[...], jnp.concatenate(lanes, axis=1), preferred_element_type=jnp.float32
-        )
+        mixed = exact(in_mat_ref[...], jnp.concatenate(lanes, axis=1))
         coarse = jnp.concatenate(
             [mixed[h * per_tile : (h + 1) * per_tile] for h in range(tiles)], axis=1
         )
-        coarse = (coarse * sign).astype(jnp.bfloat16)
         fine_ref[...] = jnp.dot(coarse, table_ref[...], preferred_element_type=jnp.float32)
         here = pl.ds(b * GROUP, GROUP)
         parts = []
@@ -146,18 +178,22 @@
             )
             value = jnp.where(p < live_ref[0], moved, dens_ref[p, here, :])
             next_ref[p, here, :] = value
+            if b == groups - 1:
+                copies[p].start()
             parts.append(value.astype(jnp.bfloat16))
         lifted = lax.dot_general(
             jnp.concatenate(parts, axis=0), table_ref[...], (((1,), (1,)), ((), ())),
             preferred_element_type=jnp.float32,
         )
-        lifted = (lifted * (sign * scale)).astype(jnp.bfloat16)
+        lifted = (lifted * scale).astype(jnp.bfloat16)
         stacked = jnp.concatenate(
             [lifted[:, h * 2 * LANES : (h + 1) * 2 * LANES] for h in range(tiles)], axis=0
         )
         ordered = exact(out_mat_ref[...], stacked)
         for g in range(2):
             send_ref[g, pl.ds(b * back, back), :] = ordered[:, g * LANES : (g + 1) * LANES]
+    for copy in copies:
+        copy.wait()
 
 
 def per_device(velocity, density, live_planes):
@@ -166,7 +202,7 @@
     slabs = depth // planes
     tiles = modes // LANES
     fine_cells = 2 * cells
-    table, sign = half_table(2 * modes, fine_cells)
+    tables = half_tables(2 * modes, fine_cells)
     sizes = dict(s=GROUP, c=comps, p=planes, h=tiles, y=GROUP)
     prep_mat = selector("shcp", "chsp", sizes)
     in_mat = selector("hcpy", "yhcp", sizes)
@@ -174,6 +210,7 @@
     chunk = comps * planes * tiles
     vmem = pl.BlockSpec(memory_space=pltpu.VMEM)
     smem = pl.BlockSpec(memory_space=pltpu.SMEM)
+    hbm = pl.BlockSpec(memory_space=pltpu.HBM)
     params = pltpu.CompilerParams(vmem_limit_bytes=(24 if rows <= GROUP else 56) * 2**20)
     f32, b16 = jnp.float32, jnp.bfloat16
 
@@ -184,8 +221,14 @@
             jax.ShapeDtypeStruct(density.shape, b16),
             jax.ShapeDtypeStruct((planes, rows, LANES), f32),
         ),
-        in_specs=[vmem] * 3,
+        in_specs=[hbm] * 3,
         out_specs=(vmem,) * 3,
+        scratch_shapes=[
+            pltpu.VMEM((comps, depth, modes), b16),
+            pltpu.VMEM(density.shape, f32),
+            pltpu.VMEM(prep_mat.shape, b16),
+            pltpu.SemaphoreType.DMA((3,)),
+        ],
         compiler_params=params,
         name="prepare",
     )(velocity.reshape(comps, depth, modes), density, prep_mat)
@@ -199,29 +242,38 @@
     recv = lax.all_to_all(send.reshape(2 * slabs, chunk, LANES), ALL, 0, 0, tiled=True)
     recv = recv.reshape(2, slabs * chunk, LANES)
 
+    side = lax.axis_index("grp").reshape(1)
     field = jax.ShapeDtypeStruct(density.shape, f32)
-    grads = pl.pallas_call(
+    *grads, table, in_mat, out_mat = pl.pallas_call(
         stencil_kernel,
-        out_shape=(field,) * 4,
-        in_specs=[vmem] * 4,
-        out_specs=(vmem,) * 4,
-        scratch_shapes=[pltpu.VMEM((3 * planes, rows, cells), f32)],
+        out_shape=(field,) * 5 + tuple(
+            jax.ShapeDtypeStruct(m.shape, b16) for m in (tables[0], in_mat, out_mat)
+        ),
+        in_specs=[smem, hbm, vmem, vmem, vmem, hbm, hbm, hbm],
+        out_specs=(vmem,) * 8,
+        scratch_shapes=[
+            pltpu.VMEM((3 * planes, rows, cells), f32), pltpu.SemaphoreType.DMA((4,))
+        ],
         compiler_params=params,
-        cost_estimate=pl.CostEstimate(flops=60 * density.size, bytes_accessed=24 * density.size, transcendentals=0),
+        cost_estimate=pl.CostEstimate(flops=STENCIL_FLOPS, bytes_accessed=24 * density.size, transcendentals=0),
         name="stencil",
-    )(density, low, high, other)
-
-    side = lax.axis_index("grp").reshape(1)
+    )(side, density, low, high, other, tables, in_mat, out_mat)
+    gx, gy, gz, base, dens = grads
+
     scale = -math.sqrt(2.0 / fine_cells)
     density_next, back = pl.pallas_call(
         functools.partial(advance_kernel, scale),
         out_shape=(field, jax.ShapeDtypeStruct((2, rows * planes * tiles, LANES), b16)),
-        in_specs=[smem, smem] + [vmem] * 10,
-        out_specs=(vmem,) * 2,
-        scratch_shapes=[pltpu.VMEM((comps * planes * GROUP, cells), f32)],
+        in_specs=[smem] + [vmem] * 9,
+        out_specs=(hbm, vmem),
+        scratch_shapes=[
+            pltpu.VMEM((comps * planes * GROUP, cells), f32),
+            pltpu.VMEM(density.shape, f32),
+            pltpu.SemaphoreType.DMA((planes,)),
+        ],
         compiler_params=params,
         name="advance",
-    )(live_planes, side, recv, table, sign, in_mat, out_mat, density, *grads)
+    )(live_planes, recv, table, in_mat, out_mat, dens, gx, gy, gz, base)
 
     home = lax.all_to_all(back.reshape(2 * rows, planes * tiles, LANES), ALL, 0, 0, tiled=True)
     home = home.reshape(2, slabs * planes * tiles, LANES).astype(f32)

time: 41.3 us -> 39.3 us (0.952)
  waiting for transfers between devices: 9.23 us -> 3.41 us
  local copies, waits for them, and re-layouts: 4.69 us -> 7.06 us
  blocking collectives: 9 us -> 9.58 us
  Pallas kernels: 3.19 us -> 3.66 us
    ppermute x1, waiting for transfers between devices: 5.99 us -> 1.78 us  [per_device(): low = lax.ppermute(dens16, ('row', 'col'), forward)]
    ppermute x1, waiting for transfers between devices: 2.69 us -> 0.01 us  [per_device(): high = lax.ppermute(dens16, ('row', 'col'), backward)]
    unnamed x16 -> x14, local copies, waits for them, and re-layouts: 4.69 us -> 7.06 us
    all_to_all x1, waiting for transfers between devices: 0.01 us -> 1.62 us  [per_device(): lax.all_to_all(send.reshape(2 * slabs, chunk, LANES), ALL, 0, 0, tiled=True)]
    ppermute x1, starting transfers between devices: 5.52 us -> 6.99 us  [per_device(): high = lax.ppermute(dens16, ('row', 'col'), backward)]
    all_to_all x1, starting transfers between devices: 7.3 us -> 6.1 us  [per_device(): lax.all_to_all(send.reshape(2 * slabs, chunk, LANES), ALL, 0, 0, tiled=True)]
    all_to_all x1, blocking collectives: 9 us -> 9.58 us  [per_device(): lax.all_to_all(back.reshape(2 * rows, planes * tiles, LANES), ALL, 0, 0,...]
    ppermute x1, waiting for transfers between devices: 0.55 us -> 0.01 us  [per_device(): other = lax.ppermute(edge, 'grp', [(0, 1), (1, 0)])]
  transfers between devices with their start and end apart: 4 -> 4, of which waited for: 3 -> 2; matrix products, arithmetic and copies ran while one was open for 0% -> 0% of each run, Pallas kernels for 2% -> 3%
where the time goes in v2:
time: 39.3 us; the launch traced here: 38.8 us
  starting transfers between devices  13.1 us (33%)
  blocking collectives  9.58 us (24%)
  local copies, waits for them, and re-layouts  7.06 us (18%)
  Pallas kernels  3.66 us (9%)
  waiting for transfers between devices  3.41 us (9%)
  between operations  1.35 us (3%)
  other arithmetic  0.65 us (2%)
    all_to_all x1, blocking collectives, per_device(): lax.all_to_all(back.reshape(2 * rows, planes * tiles, LANES), ALL, 0, 0,...  9.58 us
    unnamed x14, local copies, waits for them, and re-layouts  7.06 us
    ppermute x1, starting transfers between devices, per_device(): high = lax.ppermute(dens16, ('row', 'col'), backward)  6.99 us
    all_to_all x1, starting transfers between devices, per_device(): lax.all_to_all(send.reshape(2 * slabs, chunk, LANES), ALL, 0, 0, tiled=True)  6.1 us
    ppermute x1, waiting for transfers between devices, per_device(): low = lax.ppermute(dens16, ('row', 'col'), forward)  1.78 us
    all_to_all x1, waiting for transfers between devices, per_device(): lax.all_to_all(send.reshape(2 * slabs, chunk, LANES), ALL, 0, 0, tiled=True)  1.62 us
    pallas_call x1, Pallas kernels, per_device(): pl.pallas_call(functools.partial(advance_kernel, scale), out_shape=(field...  1.43 us
    pallas_call x1, Pallas kernels, per_device(): pl.pallas_call(functools.partial(prepare_kernel, planes), out_shape=(jax....  1.16 us
  transfers between devices with their start and end apart: 4, of which 2 were waited for; matrix products, arithmetic and copies ran while one was open for 0% of the time, Pallas kernels for 3%

profile of v2, /device:TPU:0, one launch (start us, length us, event | category | flops | bytes accessed | tf_op | source)
XLA Modules:
  0.0 38.8 jit_solution(606787650768758156)
XLA Ops:
  0.6 0.0 copy-start
  0.6 1.0 %copy-done = bf16[384,384]{1,0:T(8,128)(2,1)S(1)} copy-done((bf16[384,384]{1,0:T(8,128)(2,1)S(1)}, bf16[384,384]{1,0:T(8,128)(2,1)}, u32[]{:S(2)}) %copy-start) | copy-done | bytes 294936
  1.6 0.0 copy-start.1
  1.6 0.9 %copy-done.1 = f32[4,16,1024]{2,1,0:T(8,128)S(1)} copy-done((f32[4,16,1024]{2,1,0:T(8,128)S(1)}, f32[4,16,1024]{2,1,0:T(8,128)}, u32[]{:S(2)}) %copy-start.1) | copy-done | bytes 262168
  2.5 0.0 copy-start.3
  2.5 0.9 %copy-done.3 = bf16[3,64,1,256]{3,1,2,0:T(8,128)(2,1)S(1)} copy-done((bf16[3,64,1,256]{3,1,2,0:T(8,128)(2,1)S(1)}, bf16[3,64,1,256]{3,1,2,0:T(8,128)(2,1)}, u32[]{:S(2)}) %copy-start.3) | copy-done | bytes 98328
  3.4 1.2 %prepare.1 = (bf16[2,384,128]{2,1,0:T(8,128)(2,1)}, bf16[4,16,1024]{2,1,0:T(8,128)(2,1)S(1)}, f32[4,16,128]{2,1,0:T(8,128)S(1)}) custom-call(bf16[3,64,256]{2,1,0:T(8,128)(2,1)S(1)} %bitcast.7, f32[4,16,1024]{2,1,0:T(8,128)S(1)} %copy-done.1, bf16[384,384]{1,0:T(8,128)(2,1)S(1)} %copy-done), custom_call_target="tpu_custom_call" | custom-call | tf_op jit(solution)/shard_map/prepare/pallas_call | solution.py:217
  4.6 7.0 %collective-permute-start.1 = (bf16[4,16,1024]{2,1,0:T(8,128)(2,1)S(1)}, bf16[4,16,1024]{2,1,0:T(8,128)(2,1)S(1)}, u32[]{:S(2)}, u32[]{:S(2)}) collective-permute-start(bf16[4,16,1024]{2,1,0:T(8,128)(2,1)S(1)} %get-tuple-element.16), channel_id=1, source_target_pairs={{1,0},{2,1},{3,2},{4,3},{5,4},{6,5},{7,6},{8,7},{9,8},{10,9},{11,1... | collective-permute-start | bytes 393224 | tf_op jit(solution)/shard_map/ppermute | solution.py:241
  11.6 0.0 collective-permute-start
  11.6 0.0 collective-permute-start.2
  11.6 6.1 %all-to-all-start = ((bf16[32,24,128]{2,1,0:T(8,128)(2,1)}), bf16[32,24,128]{2,1,0:T(8,128)(2,1)S(1)}, u32[]{:S(2)}, u32[]{:S(2)}) async-start(bf16[32,24,128]{2,1,0:T(8,128)(2,1)} %bitcast.1), calls=%async_computation | async-start | bytes 393216 | tf_op jit(solution)/shard_map/all_to_all | solution.py:242
  18.4 0.0 collective-permute-done.2.edge_ref
  18.4 0.0 collective-permute-done.1.high_ref
  18.4 1.8 %collective-permute-done.low_ref = bf16[4,16,1024]{2,1,0:T(8,128)(2,1)S(1)} collective-permute-done((bf16[4,16,1024]{2,1,0:T(8,128)(2,1)S(1)}, bf16[4,16,1024]{2,1,0:T(8,128)(2,1)S(1)}, u32[]{:S(2)}, u32[]{:S(2)}) %collective-permute-start) | collective-permute-done | bytes 131104 | tf_op jit(solution)/shard_map/ppermute | solution.py:240
  20.2 0.0 copy-start.2
  20.2 0.9 %copy-done.2 = f32[4,16,1024]{2,1,0:T(8,128)S(1)} copy-done((f32[4,16,1024]{2,1,0:T(8,128)S(1)}, f32[4,16,1024]{2,1,0:T(8,128)}, u32[]{:S(2)}) %copy-start.2) | copy-done | bytes 262168
  21.1 0.0 copy-start.4
  21.1 1.6 %copy-done.4 = bf16[2,512,1024]{2,1,0:T(8,128)(2,1)S(1)} copy-done((bf16[2,512,1024]{2,1,0:T(8,128)(2,1)S(1)}, bf16[2,512,1024]{2,1,0:T(8,128)(2,1)}, u32[]{:S(2)}) %copy-start.4) | copy-done | bytes 2097176
  22.7 0.0 copy-start.5
  22.7 1.0 %copy-done.5 = bf16[384,384]{1,0:T(8,128)(2,1)S(1)} copy-done((bf16[384,384]{1,0:T(8,128)(2,1)S(1)}, bf16[384,384]{1,0:T(8,128)(2,1)}, u32[]{:S(2)}) %copy-start.5) | copy-done | bytes 294936
  23.7 0.0 copy-start.6
  23.7 0.8 %copy-done.6 = bf16[128,128]{1,0:T(8,128)(2,1)S(1)} copy-done((bf16[128,128]{1,0:T(8,128)(2,1)S(1)}, bf16[128,128]{1,0:T(8,128)(2,1)}, u32[]{:S(2)}) %copy-start.6) | copy-done | bytes 32792
  24.4 1.1 %stencil.1 = (f32[4,16,1024]{2,1,0:T(8,128)S(1)}, f32[4,16,1024]{2,1,0:T(8,128)S(1)}, f32[4,16,1024]{2,1,0:T(8,128)S(1)}, f32[4,16,1024]{2,1,0:T(8,128)S(1)}, f3...) custom-call(s32[1]{0:T(128)} %bitcast.3.side_ref, ...), custom_call_target="tpu_custom_call" | custom-call | flops 20000000000 | bytes 1572864 | tf_op jit(solution)/shard_map/stencil/pallas_call | solution.py:247
  25.5 1.6 %all-to-all-done = bf16[32,24,128]{2,1,0:T(8,128)(2,1)S(1)} async-done(((bf16[32,24,128]{2,1,0:T(8,128)(2,1)}), bf16[32,24,128]{2,1,0:T(8,128)(2,1)S(1)}, u32[]{:S(2)}, u32[]{:S(2)}) %all-to-all-start) | async-done | bytes 196640 | tf_op jit(solution)/shard_map/all_to_all | solution.py:242
  27.1 1.4 %advance.1 = (f32[4,16,1024]{2,1,0:T(8,128)}, bf16[2,128,128]{2,1,0:T(8,128)(2,1)S(1)}) custom-call(s32[1]{0:T(128)S(6)} %copy.9.live_ref, bf16[2,384,128]{2,1,0:T(8,128)(2,1)S(1)} %bitcast.6, bf16[512,1024]{1,0:T(8,128)(2,1)S(1)} %get-tuple-element.18.table_ref, bf16[384,384]{1,0:T(8,128)(2,1)S(1)} %get-tuple-element.19.in_mat_ref, ...), custom_call_target="tpu_custom_call" | custom-call | tf_op jit(solution)/shard_map/advance/pallas_call | solution.py:264
  28.6 9.6 %all_to_all.10 = bf16[32,8,128]{2,1,0:T(8,128)(2,1)S(1)} all-to-all(bf16[32,8,128]{2,1,0:T(8,128)(2,1)S(1)} %bitcast.8), channel_id=1, replica_groups=mesh['grp'=2,'row'=4,'col'=4] {'grp','row','col'}, dimensions={0} | all-to-all | bytes 131072 | tf_op jit(solution)/shard_map/all_to_all | solution.py:278
  38.2 0.6 %slice_add_fusion = f32[16,8,128]{2,1,0:T(8,128)} fusion(f32[32,8,128]{2,1,0:T(8,128)S(1)} %convert_element_type.4), kind=kLoop, calls=%fused_computation | loop fusion | flops 16384 | bytes 196608 | tf_op jit(solution)/shard_map/add | solution.py:280
  (1 shorter events, 0.0 us)
Async XLA Ops:
  0.6 1.0 %copy-start = (bf16[384,384]{1,0:T(8,128)(2,1)S(1)}, bf16[384,384]{1,0:T(8,128)(2,1)}, u32[]{:S(2)}) copy-start(bf16[384,384]{1,0:T(8,128)(2,1)} %constant.14.clone.mat_hbm) | copy-start | bytes 884740
  1.6 0.9 %copy-start.1 = (f32[4,16,1024]{2,1,0:T(8,128)S(1)}, f32[4,16,1024]{2,1,0:T(8,128)}, u32[]{:S(2)}) copy-start(f32[4,16,1024]{2,1,0:T(8,128)} %dens_hbm.3) | copy-start | bytes 786436
  2.5 0.9 %copy-start.3 = (bf16[3,64,1,256]{3,1,2,0:T(8,128)(2,1)S(1)}, bf16[3,64,1,256]{3,1,2,0:T(8,128)(2,1)}, u32[]{:S(2)}) copy-start(bf16[3,64,1,256]{3,1,2,0:T(8,128)(2,1)} %param.7) | copy-start | bytes 294916
  4.6 13.8 %collective-permute-start.1 = (bf16[4,16,1024]{2,1,0:T(8,128)(2,1)S(1)}, bf16[4,16,1024]{2,1,0:T(8,128)(2,1)S(1)}, u32[]{:S(2)}, u32[]{:S(2)}) collective-permute-start(bf16[4,16,1024]{2,1,0:T(8,128)(2,1)S(1)} %get-tuple-element.16), channel_id=1, source_target_pairs={{1,0},{2,1},{3,2},{4,3},{5,4},{6,5},{7,6},{8,7},{9,8},{10,9},{11,1... | collective-permute-start | bytes 393224 | tf_op jit(solution)/shard_map/ppermute | solution.py:241
  11.6 8.6 %collective-permute-start = (bf16[4,16,1024]{2,1,0:T(8,128)(2,1)S(1)}, bf16[4,16,1024]{2,1,0:T(8,128)(2,1)S(1)}, u32[]{:S(2)}, u32[]{:S(2)}) collective-permute-start(bf16[4,16,1024]{2,1,0:T(8,128)(2,1)S(1)} %get-tuple-element.16), channel_id=1, source_target_pairs={{0,1},{1,2},{2,3},{3,4},{4,5},{5,6},{6,7},{7,8},{8,9},{9,10},{10,1... | collective-permute-start | bytes 393224 | tf_op jit(solution)/shard_map/ppermute | solution.py:240
  11.6 6.8 %collective-permute-start.2 = (f32[4,16,128]{2,1,0:T(8,128)S(1)}, f32[4,16,128]{2,1,0:T(8,128)S(1)}, u32[]{:S(2)}, u32[]{:S(2)}) collective-permute-start(f32[4,16,128]{2,1,0:T(8,128)S(1)} %get-tuple-element.17), channel_id=1, source_target_pairs={{0,16},{16,0},{1,17},{17,1},{2,18},{18,2},{3,19},{19,3},{4,20},{20... | collective-permute-start | bytes 98312 | tf_op jit(solution)/shard_map/ppermute | solution.py:239
  11.6 15.5 %all-to-all-start = ((bf16[32,24,128]{2,1,0:T(8,128)(2,1)}), bf16[32,24,128]{2,1,0:T(8,128)(2,1)S(1)}, u32[]{:S(2)}, u32[]{:S(2)}) async-start(bf16[32,24,128]{2,1,0:T(8,128)(2,1)} %bitcast.1), calls=%async_computation | async-start | bytes 393216 | tf_op jit(solution)/shard_map/all_to_all | solution.py:242
  20.2 1.0 %copy-start.2 = (f32[4,16,1024]{2,1,0:T(8,128)S(1)}, f32[4,16,1024]{2,1,0:T(8,128)}, u32[]{:S(2)}) copy-start(f32[4,16,1024]{2,1,0:T(8,128)} %dens_hbm.3) | copy-start | bytes 786436
  21.1 1.6 %copy-start.4 = (bf16[2,512,1024]{2,1,0:T(8,128)(2,1)S(1)}, bf16[2,512,1024]{2,1,0:T(8,128)(2,1)}, u32[]{:S(2)}) copy-start(bf16[2,512,1024]{2,1,0:T(8,128)(2,1)} %constant.15.clone.table_hbm) | copy-start | bytes 6291460
  22.7 1.0 %copy-start.5 = (bf16[384,384]{1,0:T(8,128)(2,1)S(1)}, bf16[384,384]{1,0:T(8,128)(2,1)}, u32[]{:S(2)}) copy-start(bf16[384,384]{1,0:T(8,128)(2,1)} %constant.16.clone.in_hbm) | copy-start | bytes 884740
  23.7 0.8 %copy-start.6 = (bf16[128,128]{1,0:T(8,128)(2,1)S(1)}, bf16[128,128]{1,0:T(8,128)(2,1)}, u32[]{:S(2)}) copy-start(bf16[128,128]{1,0:T(8,128)(2,1)} %constant.17.clone.out_hbm) | copy-start | bytes 98308

commit v3 on v2

--- a/solution.py
+++ b/solution.py
@@ -45,6 +45,10 @@
 
 def exact(matrix, rows):
     return jnp.dot(matrix, rows, preferred_element_type=jnp.float32).astype(jnp.bfloat16)
+
+
+def keep(array):
+    return pltpu.with_memory_space_constraint(array, pltpu.HBM)
 
 
 def prepare_kernel(
@@ -84,7 +88,7 @@
 
 
 def stencil_kernel(
-    side_ref, dens_hbm, low_ref, high_ref, edge_ref, table_hbm, in_hbm, out_hbm,
+    dens_hbm, near_ref, far_ref, edge_ref, table_hbm, in_hbm, out_hbm,
     gx_ref, gy_ref, gz_ref, base_ref, field_ref, table_ref, in_ref, out_ref, zz_ref, sems,
 ):
     planes, rows, cells = dens_hbm.shape
@@ -92,15 +96,16 @@
         pltpu.make_async_copy(source, target, sems.at[i])
         for i, (source, target) in enumerate(
             [
-                (dens_hbm, field_ref), (table_hbm.at[side_ref[0]], table_ref),
+                (dens_hbm, field_ref), (table_hbm.at[lax.axis_index("grp")], table_ref),
                 (in_hbm, in_ref), (out_hbm, out_ref),
             ]
         )
     ]
     for copy in copies:
         copy.start()
-    zz_ref[pl.ds(0, planes)] = low_ref[...].astype(jnp.float32)
-    zz_ref[pl.ds(2 * planes, planes)] = high_ref[...].astype(jnp.float32)
+    odd = lax.axis_index(("row", "col")) % 2
+    zz_ref[pl.ds(2 * planes * (1 - odd), planes)] = near_ref[...].astype(jnp.float32)
+    zz_ref[pl.ds(2 * planes * odd, planes)] = far_ref[...].astype(jnp.float32)
     copies[0].wait()
     zz_ref[pl.ds(planes, planes)] = field_ref[...]
 
@@ -231,25 +236,24 @@
         ],
         compiler_params=params,
         name="prepare",
-    )(velocity.reshape(comps, depth, modes), density, prep_mat)
+    )(keep(velocity.reshape(comps, depth, modes)), keep(density), keep(prep_mat))
 
     count = slabs
-    forward = [(i, (i + 1) % count) for i in range(count)]
-    backward = [(target, source) for source, target in forward]
+    even_first = [(i, i ^ 1) for i in range(count)]
+    odd_first = [((i + 1) % count, ((i ^ 1) + 1) % count) for i in range(count)]
+    far = lax.ppermute(dens16, ("row", "col"), odd_first)
+    near = lax.ppermute(dens16, ("row", "col"), even_first)
     other = lax.ppermute(edge, "grp", [(0, 1), (1, 0)])
-    low = lax.ppermute(dens16, ("row", "col"), forward)
-    high = lax.ppermute(dens16, ("row", "col"), backward)
     recv = lax.all_to_all(send.reshape(2 * slabs, chunk, LANES), ALL, 0, 0, tiled=True)
     recv = recv.reshape(2, slabs * chunk, LANES)
 
-    side = lax.axis_index("grp").reshape(1)
     field = jax.ShapeDtypeStruct(density.shape, f32)
     *grads, table, in_mat, out_mat = pl.pallas_call(
         stencil_kernel,
         out_shape=(field,) * 5 + tuple(
             jax.ShapeDtypeStruct(m.shape, b16) for m in (tables[0], in_mat, out_mat)
         ),
-        in_specs=[smem, hbm, vmem, vmem, vmem, hbm, hbm, hbm],
+        in_specs=[hbm, vmem, vmem, vmem, hbm, hbm, hbm],
         out_specs=(vmem,) * 8,
         scratch_shapes=[
             pltpu.VMEM((3 * planes, rows, cells), f32), pltpu.SemaphoreType.DMA((4,))
@@ -257,7 +261,7 @@
         compiler_params=params,
         cost_estimate=pl.CostEstimate(flops=STENCIL_FLOPS, bytes_accessed=24 * density.size, transcendentals=0),
         name="stencil",
-    )(side, density, low, high, other, tables, in_mat, out_mat)
+    )(keep(density), near, far, other, keep(tables), keep(in_mat), keep(out_mat))
     gx, gy, gz, base, dens = grads
 
     scale = -math.sqrt(2.0 / fine_cells)

time: 39.3 us -> 33.7 us (0.86)
  local copies, waits for them, and re-layouts: 7.06 us -> 0 us
  waiting for transfers between devices: 3.41 us -> 6.97 us
  starting transfers between devices: 13.1 us -> 9.59 us
  Pallas kernels: 3.66 us -> 5.24 us
    unnamed x14 -> x0, local copies, waits for them, and re-layouts: 7.06 us -> none
    all_to_all x1, starting transfers between devices: 6.1 us -> 2.58 us  [per_device(): lax.all_to_all(send.reshape(2 * slabs, chunk, LANES), ALL, 0, 0, tiled=True)]
    all_to_all x1, waiting for transfers between devices: 1.62 us -> 3.51 us  [per_device(): lax.all_to_all(send.reshape(2 * slabs, chunk, LANES), ALL, 0, 0, tiled=True)]
    ppermute x2, waiting for transfers between devices: 1.78 us -> 3.46 us  [the longest x1 2.34 us: per_device(): near = lax.ppermute(dens16, ('row', 'col'), even_first)]
    pallas_call x1, Pallas kernels: 1.16 us -> 2.03 us  [per_device(): pl.pallas_call(functools.partial(prepare_kernel, planes), out_shape=(jax....]
    pallas_call x1, Pallas kernels: 1.06 us -> 1.77 us  [per_device(): pl.pallas_call(stencil_kernel, out_shape=(field,) * 5 + tuple((jax.ShapeD...]
  transfers between devices with their start and end apart: 4 -> 4, of which waited for: 2 -> 3; matrix products, arithmetic and copies ran while one was open for 0% -> 0% of each run, Pallas kernels for 3% -> 5%
where the time goes in v3:
time: 33.7 us; the launch traced here: 33.5 us
  blocking collectives  9.69 us (29%)
  starting transfers between devices  9.59 us (28%)
  waiting for transfers between devices  6.97 us (21%)
  Pallas kernels  5.24 us (16%)
  between operations  1.32 us (4%)
  other arithmetic  0.65 us (2%)
    all_to_all x1, blocking collectives, per_device(): lax.all_to_all(back.reshape(2 * rows, planes * tiles, LANES), ALL, 0, 0,...  9.69 us
    ppermute x1, starting transfers between devices, per_device(): far = lax.ppermute(dens16, ('row', 'col'), odd_first)  7 us
    all_to_all x1, waiting for transfers between devices, per_device(): lax.all_to_all(send.reshape(2 * slabs, chunk, LANES), ALL, 0, 0, tiled=True)  3.51 us
    all_to_all x1, starting transfers between devices, per_device(): lax.all_to_all(send.reshape(2 * slabs, chunk, LANES), ALL, 0, 0, tiled=True)  2.58 us
    ppermute x1, waiting for transfers between devices, per_device(): near = lax.ppermute(dens16, ('row', 'col'), even_first)  2.34 us
    pallas_call x1, Pallas kernels, per_device(): pl.pallas_call(functools.partial(prepare_kernel, planes), out_shape=(jax....  2.03 us
    pallas_call x1, Pallas kernels, per_device(): pl.pallas_call(stencil_kernel, out_shape=(field,) * 5 + tuple((jax.ShapeD...  1.77 us
    pallas_call x1, Pallas kernels, per_device(): pl.pallas_call(functools.partial(advance_kernel, scale), out_shape=(field...  1.43 us
  transfers between devices with their start and end apart: 4, of which 3 were waited for; matrix products, arithmetic and copies ran while one was open for 0% of the time, Pallas kernels for 5%

profile of v3, /device:TPU:0, one launch (start us, length us, event | category | flops | bytes accessed | tf_op | source)
XLA Modules:
  0.0 33.5 jit_solution(11086194766586947542)
XLA Ops:
  0.6 2.0 %prepare.1 = (bf16[2,384,128]{2,1,0:T(8,128)(2,1)}, bf16[4,16,1024]{2,1,0:T(8,128)(2,1)S(1)}, f32[4,16,128]{2,1,0:T(8,128)S(1)}) custom-call(bf16[3,64,256]{2,1,0:T(8,128)(2,1)} %bitcast.7, f32[4,16,1024]{2,1,0:T(8,128)} %dens_hbm.3, bf16[384,384]{1,0:T(8,128)(2,1)} %constant.8.clone.mat_hbm), custom_call_target="tpu_custom_call" | custom-call | tf_op jit(solution)/shard_map/prepare/pallas_call | solution.py:222
  2.7 7.0 %collective-permute-start.1 = (bf16[4,16,1024]{2,1,0:T(8,128)(2,1)S(1)}, bf16[4,16,1024]{2,1,0:T(8,128)(2,1)S(1)}, u32[]{:S(2)}, u32[]{:S(2)}) collective-permute-start(bf16[4,16,1024]{2,1,0:T(8,128)(2,1)S(1)} %get-tuple-element.16), channel_id=1, source_target_pairs={{1,2},{2,1},{3,4},{4,3},{5,6},{6,5},{7,8},{8,7},{9,10},{10,9},{11,... | collective-permute-start | bytes 393224 | tf_op jit(solution)/shard_map/ppermute | solution.py:244
  9.7 0.0 collective-permute-start
  9.7 0.0 collective-permute-start.2
  9.7 2.6 %all-to-all-start = ((bf16[32,24,128]{2,1,0:T(8,128)(2,1)}), bf16[32,24,128]{2,1,0:T(8,128)(2,1)S(1)}, u32[]{:S(2)}, u32[]{:S(2)}) async-start(bf16[32,24,128]{2,1,0:T(8,128)(2,1)} %bitcast.1), calls=%async_computation | async-start | bytes 393216 | tf_op jit(solution)/shard_map/all_to_all | solution.py:247
  12.9 0.0 collective-permute-done.2.edge_ref
  12.9 1.1 %collective-permute-done.1.far_ref = bf16[4,16,1024]{2,1,0:T(8,128)(2,1)S(1)} collective-permute-done((bf16[4,16,1024]{2,1,0:T(8,128)(2,1)S(1)}, bf16[4,16,1024]{2,1,0:T(8,128)(2,1)S(1)}, u32[]{:S(2)}, u32[]{:S(2)}) %collective-permute-start.1) | collective-permute-done | bytes 131104 | tf_op jit(solution)/shard_map/ppermute | solution.py:244
  14.0 2.3 %collective-permute-done.near_ref = bf16[4,16,1024]{2,1,0:T(8,128)(2,1)S(1)} collective-permute-done((bf16[4,16,1024]{2,1,0:T(8,128)(2,1)S(1)}, bf16[4,16,1024]{2,1,0:T(8,128)(2,1)S(1)}, u32[]{:S(2)}, u32[]{:S(2)}) %collective-permute-start) | collective-permute-done | bytes 131104 | tf_op jit(solution)/shard_map/ppermute | solution.py:245
  16.4 1.8 %stencil.1 = (f32[4,16,1024]{2,1,0:T(8,128)S(1)}, f32[4,16,1024]{2,1,0:T(8,128)S(1)}, f32[4,16,1024]{2,1,0:T(8,128)S(1)}, f32[4,16,1024]{2,1,0:T(8,128)S(1)}, f3...) custom-call(f32[4,16,1024]{2,1,0:T(8,128)} %dens_hbm.3, ...), custom_call_target="tpu_custom_call" | custom-call | flops 20000000000 | bytes 1572864 | tf_op jit(solution)/shard_map/stencil/pallas_call | solution.py:251
  18.2 3.5 %all-to-all-done = bf16[32,24,128]{2,1,0:T(8,128)(2,1)S(1)} async-done(((bf16[32,24,128]{2,1,0:T(8,128)(2,1)}), bf16[32,24,128]{2,1,0:T(8,128)(2,1)S(1)}, u32[]{:S(2)}, u32[]{:S(2)}) %all-to-all-start) | async-done | bytes 196640 | tf_op jit(solution)/shard_map/all_to_all | solution.py:247
  21.7 1.4 %advance.1 = (f32[4,16,1024]{2,1,0:T(8,128)}, bf16[2,128,128]{2,1,0:T(8,128)(2,1)S(1)}) custom-call(s32[1]{0:T(128)S(6)} %copy.9.live_ref, bf16[2,384,128]{2,1,0:T(8,128)(2,1)S(1)} %bitcast.5, bf16[512,1024]{1,0:T(8,128)(2,1)S(1)} %get-tuple-element.18.table_ref, bf16[384,384]{1,0:T(8,128)(2,1)S(1)} %get-tuple-element.19.in_mat_ref, ...), custom_call_target="tpu_custom_call" | custom-call | tf_op jit(solution)/shard_map/advance/pallas_call | solution.py:268
  23.1 9.7 %all_to_all.10 = bf16[32,8,128]{2,1,0:T(8,128)(2,1)S(1)} all-to-all(bf16[32,8,128]{2,1,0:T(8,128)(2,1)S(1)} %bitcast.6), channel_id=1, replica_groups=mesh['grp'=2,'row'=4,'col'=4] {'grp','row','col'}, dimensions={0} | all-to-all | bytes 131072 | tf_op jit(solution)/shard_map/all_to_all | solution.py:282
  32.8 0.6 %slice_add_fusion = f32[16,8,128]{2,1,0:T(8,128)} fusion(f32[32,8,128]{2,1,0:T(8,128)S(1)} %convert_element_type.4), kind=kLoop, calls=%fused_computation | loop fusion | flops 16384 | bytes 196608 | tf_op jit(solution)/shard_map/add | solution.py:284
  (1 shorter events, 0.0 us)
Async XLA Ops:
  2.7 11.4 %collective-permute-start.1 = (bf16[4,16,1024]{2,1,0:T(8,128)(2,1)S(1)}, bf16[4,16,1024]{2,1,0:T(8,128)(2,1)S(1)}, u32[]{:S(2)}, u32[]{:S(2)}) collective-permute-start(bf16[4,16,1024]{2,1,0:T(8,128)(2,1)S(1)} %get-tuple-element.16), channel_id=1, source_target_pairs={{1,2},{2,1},{3,4},{4,3},{5,6},{6,5},{7,8},{8,7},{9,10},{10,9},{11,... | collective-permute-start | bytes 393224 | tf_op jit(solution)/shard_map/ppermute | solution.py:244
  9.7 6.7 %collective-permute-start = (bf16[4,16,1024]{2,1,0:T(8,128)(2,1)S(1)}, bf16[4,16,1024]{2,1,0:T(8,128)(2,1)S(1)}, u32[]{:S(2)}, u32[]{:S(2)}) collective-permute-start(bf16[4,16,1024]{2,1,0:T(8,128)(2,1)S(1)} %get-tuple-element.16), channel_id=1, source_target_pairs={{0,1},{1,0},{2,3},{3,2},{4,5},{5,4},{6,7},{7,6},{8,9},{9,8},{10,11... | collective-permute-start | bytes 393224 | tf_op jit(solution)/shard_map/ppermute | solution.py:245
  9.7 3.2 %collective-permute-start.2 = (f32[4,16,128]{2,1,0:T(8,128)S(1)}, f32[4,16,128]{2,1,0:T(8,128)S(1)}, u32[]{:S(2)}, u32[]{:S(2)}) collective-permute-start(f32[4,16,128]{2,1,0:T(8,128)S(1)} %get-tuple-element.17), channel_id=1, source_target_pairs={{0,16},{16,0},{1,17},{17,1},{2,18},{18,2},{3,19},{19,3},{4,20},{20... | collective-permute-start | bytes 98312 | tf_op jit(solution)/shard_map/ppermute | solution.py:246
  9.7 12.0 %all-to-all-start = ((bf16[32,24,128]{2,1,0:T(8,128)(2,1)}), bf16[32,24,128]{2,1,0:T(8,128)(2,1)S(1)}, u32[]{:S(2)}, u32[]{:S(2)}) async-start(bf16[32,24,128]{2,1,0:T(8,128)(2,1)} %bitcast.1), calls=%async_computation | async-start | bytes 393216 | tf_op jit(solution)/shard_map/all_to_all | solution.py:247

commit v4 on v3

v4 whole, which is shorter than its diff:
```python
import functools
import math

import jax
import jax.numpy as jnp
import numpy as np
from jax import lax
from jax.experimental import pallas as pl
from jax.experimental.pallas import tpu as pltpu
from jax.sharding import PartitionSpec as P

first_coef = (4.0 / 5.0, -1.0 / 5.0, 4.0 / 105.0, -1.0 / 280.0)
second_coef = (8.0 / 5.0, -1.0 / 5.0, 8.0 / 315.0, -1.0 / 560.0)
centre_coef = -205.0 / 72.0
kappa_value = 0.1
step_value = 0.2
strat_value = 1.0

LANES = 128
GROUP = 16


def half_tables(mode_count, fine_cells):
    k = np.arange(mode_count)
    half = mode_count // 2
    frequency = np.where(k < half, k, k - half + 1)
    phase = frequency[:, None] * np.arange(fine_cells)[None, :] % fine_cells
    angle = phase.astype(np.float32) * np.float32(2.0 * math.pi / fine_cells)
    table = np.where((k < half)[:, None], np.cos(angle), np.sin(angle)).astype(np.float32)
    order = k.reshape(2, half // LANES, LANES).transpose(1, 0, 2).reshape(-1)
    table = table[order].reshape(mode_count, 2, fine_cells // 2).transpose(1, 0, 2)
    sign = np.where(frequency[order] % 2 == 0, 1.0, -1.0).astype(np.float32)
    return np.ascontiguousarray(table).astype(jnp.bfloat16), np.tile(sign, (8, 1))


def selector(out_axes, in_axes, sizes):
    count = math.prod(sizes[a] for a in in_axes)
    index = np.arange(count).reshape([sizes[a] for a in in_axes])
    source = index.transpose([in_axes.index(a) for a in out_axes]).reshape(-1)
    matrix = np.zeros((count, count), np.float32)
    matrix[np.arange(count), source] = 1.0
    return matrix.astype(jnp.bfloat16)


def exact(matrix, rows):
    return jnp.dot(matrix, rows, preferred_element_type=jnp.float32).astype(jnp.bfloat16)


def keep(array):
    return pltpu.with_memory_space_constraint(array, pltpu.HBM)


def copy_all(pairs, sems):
    copies = [pltpu.make_async_copy(src, dst, sems.at[i]) for i, (src, dst) in enumerate(pairs)]
    for copy in copies:
        copy.start()
    return copies


def prepare_kernel(
    planes, vel_hbm, dens_hbm, mat_hbm, send_ref, dens16_ref, vel_ref, dens_ref, mat_ref, sems
):
    copies = copy_all([(dens_hbm, dens_ref), (vel_hbm, vel_ref), (mat_hbm, mat_ref)], sems)
    comps, depth, modes = vel_ref.shape
    tiles = modes // LANES
    step = GROUP * planes
    chunk = comps * planes * tiles * GROUP // 2
    copies[0].wait()
    dens16_ref[...] = dens_ref[...].astype(jnp.bfloat16)
    copies[1].wait()
    copies[2].wait()
    for b in range(depth // step):
        parts = []
        for c in range(comps):
            rows = vel_ref[c, pl.ds(b * step, step), :]
            for h in range(tiles):
                parts.append(rows[:, h * LANES : (h + 1) * LANES])
        mixed = exact(mat_ref[...], jnp.concatenate(parts, axis=0))
        for g in range(2):
            send_ref[g, pl.ds(b * chunk, chunk), :] = mixed[g * chunk : (g + 1) * chunk]


def stencil_kernel(
    dens_hbm, other_ref, near_ref, far_ref, near_other_ref, far_other_ref,
    table_hbm, sign_hbm, in_hbm,
    gx_ref, gy_ref, gz_ref, base_ref, field_ref, table_ref, sign_ref, in_ref, zz_ref, sems,
):
    planes, rows, cells = dens_hbm.shape
    here, there = pl.ds(0, cells), pl.ds(cells, cells)
    core = lax.axis_index("grp")
    copies = copy_all(
        [
            (dens_hbm, zz_ref.at[pl.ds(planes, planes), :, here]),
            (table_hbm.at[core], table_ref), (sign_hbm, sign_ref), (in_hbm, in_ref),
        ],
        sems,
    )
    zz_ref[pl.ds(planes, planes), :, there] = other_ref[...]
    odd = lax.axis_index(("row", "col")) % 2
    near_at, far_at = pl.ds(2 * planes * (1 - odd), planes), pl.ds(2 * planes * odd, planes)
    zz_ref[near_at, :, here] = near_ref[...].astype(jnp.float32)
    zz_ref[near_at, :, there] = near_other_ref[...].astype(jnp.float32)
    zz_ref[far_at, :, here] = far_ref[...].astype(jnp.float32)
    zz_ref[far_at, :, there] = far_other_ref[...].astype(jnp.float32)
    copies[0].wait()
    span = 2 * cells
    owned = planes // 2

    def one(p):
        at = planes + owned * core + p
        field = zz_ref[at]
        field_ref[p] = field
        grad_x = grad_y = grad_z = lap = None
        for reach in range(1, 5):
            ahead_x = pltpu.roll(field, span - reach, 1)
            behind_x = pltpu.roll(field, reach, 1)
            ahead_y = pltpu.roll(field, rows - reach, 0)
            behind_y = pltpu.roll(field, reach, 0)
            ahead_z = zz_ref[at + reach]
            behind_z = zz_ref[at - reach]
            a = step_value * first_coef[reach - 1]
            b = step_value * kappa_value * second_coef[reach - 1]
            total = (ahead_x + behind_x) + (ahead_y + behind_y) + (ahead_z + behind_z)
            if reach == 1:
                grad_x = a * (ahead_x - behind_x)
                grad_y = a * (ahead_y - behind_y)
                grad_z = a * (ahead_z - behind_z) + step_value * strat_value
                lap = (1.0 + step_value * kappa_value * 3.0 * centre_coef) * field + b * total
            else:
                grad_x = grad_x + a * (ahead_x - behind_x)
                grad_y = grad_y + a * (ahead_y - behind_y)
                grad_z = grad_z + a * (ahead_z - behind_z)
                lap = lap + b * total
        gx_ref[p] = grad_x
        gy_ref[p] = grad_y
        gz_ref[p] = grad_z
        base_ref[p] = lap

    if rows <= GROUP:
        for p in range(owned):
            one(p)
    else:
        lax.fori_loop(0, owned, lambda p, _: (one(p), 0)[1], 0)
    for copy in copies[1:]:
        copy.wait()


def advance_kernel(
    scale, live_ref, recv_ref, table_ref, sign_ref, in_mat_ref,
    dens_ref, gx_ref, gy_ref, gz_ref, base_ref, mine_ref, give_ref, send_ref, fine_ref,
):
    owned, rows, span = dens_ref.shape
    cells = span // 2
    modes = table_ref.shape[0]
    tiles = modes // (2 * LANES)
    comps = 3
    chunk = comps * owned * tiles * GROUP
    per_tile = chunk // tiles
    sign = sign_ref[0:1, :]
    first_plane = owned * lax.axis_index("grp")
    for b in range(rows // GROUP):
        lanes = [recv_ref[g, pl.ds(b * chunk, chunk), :] for g in range(2)]
        mixed = jnp.dot(
            in_mat_ref[...], jnp.concatenate(lanes, axis=1), preferred_element_type=jnp.float32
        )
        coarse = jnp.concatenate(
            [mixed[h * per_tile : (h + 1) * per_tile] for h in range(tiles)], axis=1
        )
        both = jnp.concatenate([coarse, coarse * sign], axis=0).astype(jnp.bfloat16)
        fine_ref[...] = jnp.dot(both, table_ref[...], preferred_element_type=jnp.float32)
        here = pl.ds(b * GROUP, GROUP)
        parts = []
        for side, out_ref in enumerate((mine_ref, give_ref)):
            for p in range(owned):
                at = (p, here, pl.ds(side * cells, cells))
                vel = [
                    fine_ref[pl.ds(((side * comps + c) * owned + p) * GROUP, GROUP), :]
                    for c in range(comps)
                ]
                moved = base_ref[at] - (
                    vel[0] * gx_ref[at] + vel[1] * gy_ref[at] + vel[2] * gz_ref[at]
                )
                value = jnp.where(first_plane + p < live_ref[0], moved, dens_ref[at])
                out_ref[p, here, :] = value
                parts.append(value.astype(jnp.bfloat16))
        lifted = lax.dot_general(
            jnp.concatenate(parts, axis=0), table_ref[...], (((1,), (1,)), ((), ())),
            preferred_element_type=jnp.float32,
        )
        half = owned * GROUP
        lifted = scale * lifted[:half] + (scale * sign) * lifted[half:]
        for p in range(owned):
            for h in range(tiles):
                for g in range(2):
                    first = b * GROUP * 2 * owned * tiles + (g * owned + p) * tiles + h
                    send_ref[pl.ds(first, GROUP, stride=2 * owned * tiles), :] = lifted[
                        p * GROUP : (p + 1) * GROUP, (2 * h + g) * LANES : (2 * h + g + 1) * LANES
                    ]


def finish_kernel(mine_ref, got_ref, home_ref, next_hbm, buoyancy_hbm, sems):
    owned = mine_ref.shape[0]
    core = lax.axis_index("grp")
    for copy in copy_all(
        [
            (mine_ref, next_hbm.at[pl.ds(owned * core, owned)]),
            (got_ref, next_hbm.at[pl.ds(owned * (1 - core), owned)]),
            (home_ref, buoyancy_hbm),
        ],
        sems,
    ):
        copy.wait()


def per_device(velocity, density, live_planes):
    comps, depth, _, modes = velocity.shape
    planes, rows, cells = density.shape
    slabs = depth // planes
    tiles = modes // LANES
    owned = planes // 2
    fine_cells = 2 * cells
    tables, sign = half_tables(2 * modes, fine_cells)
    sizes = dict(s=GROUP, c=comps, p=owned, h=tiles, y=GROUP, g=2)
    prep_mat = selector("gshcp", "chsgp", sizes)
    in_mat = selector("hcpy", "yhcp", sizes)
    chunk = comps * owned * tiles
    vmem = pl.BlockSpec(memory_space=pltpu.VMEM)
    smem = pl.BlockSpec(memory_space=pltpu.SMEM)
    hbm = pl.BlockSpec(memory_space=pltpu.HBM)
    params = pltpu.CompilerParams(vmem_limit_bytes=(24 if rows <= GROUP else 56) * 2**20)
    f32, b16 = jnp.float32, jnp.bfloat16

    send, dens16 = pl.pallas_call(
        functools.partial(prepare_kernel, planes),
        out_shape=(
            jax.ShapeDtypeStruct((2, slabs * chunk, LANES), b16),
            jax.ShapeDtypeStruct(density.shape, b16),
        ),
        in_specs=[hbm] * 3,
        out_specs=(vmem,) * 2,
        scratch_shapes=[
            pltpu.VMEM((comps, depth, modes), b16),
            pltpu.VMEM(density.shape, f32),
            pltpu.VMEM(prep_mat.shape, b16),
            pltpu.SemaphoreType.DMA((3,)),
        ],
        compiler_params=params,
        name="prepare",
    )(keep(velocity.reshape(comps, depth, modes)), keep(density), keep(prep_mat))

    count = slabs
    even_first = [(i, i ^ 1) for i in range(count)]
    odd_first = [((i + 1) % count, ((i ^ 1) + 1) % count) for i in range(count)]
    pair = [(0, 1), (1, 0)]
    far = lax.ppermute(dens16, ("row", "col"), odd_first)
    near = lax.ppermute(dens16, ("row", "col"), even_first)
    other = lax.ppermute(density, "grp", pair)
    far_other = lax.ppermute(far, "grp", pair)
    near_other = lax.ppermute(near, "grp", pair)
    recv = lax.all_to_all(
        send.reshape(2 * slabs, chunk // 4, 4, LANES), ("grp", "row", "col"), 0, 0, tiled=True
    )
    recv = recv.reshape(2, slabs * chunk, LANES)

    field = jax.ShapeDtypeStruct((owned, rows, fine_cells), f32)
    *grads, table, sign, in_mat = pl.pallas_call(
        stencil_kernel,
        out_shape=(field,) * 5 + (
            jax.ShapeDtypeStruct(tables[0].shape, b16),
            jax.ShapeDtypeStruct(sign.shape, f32),
            jax.ShapeDtypeStruct(in_mat.shape, b16),
        ),
        in_specs=[hbm] + [vmem] * 5 + [hbm] * 3,
        out_specs=(vmem,) * 8,
        scratch_shapes=[
            pltpu.VMEM((3 * planes, rows, fine_cells), f32), pltpu.SemaphoreType.DMA((4,))
        ],
        compiler_params=params,
        cost_estimate=pl.CostEstimate(
            flops=16 * density.size, bytes_accessed=24 * density.size, transcendentals=0
        ),
        name="stencil",
    )(
        keep(density), other, near, far, near_other, far_other,
        keep(tables), keep(sign), keep(in_mat),
    )
    gx, gy, gz, base, dens = grads

    scale = -math.sqrt(2.0 / fine_cells)
    half_field = jax.ShapeDtypeStruct((owned, rows, cells), f32)
    mine, give, back = pl.pallas_call(
        functools.partial(advance_kernel, scale),
        out_shape=(
            half_field, half_field,
            jax.ShapeDtypeStruct((rows * 2 * owned * tiles, LANES), f32),
        ),
        in_specs=[smem] + [vmem] * 9,
        out_specs=(vmem,) * 3,
        scratch_shapes=[pltpu.VMEM((2 * comps * owned * GROUP, cells), f32)],
        compiler_params=params,
        name="advance",
    )(live_planes, recv, table, sign, in_mat, dens, gx, gy, gz, base)

    home = lax.all_to_all(
        back.reshape(2 * rows * owned, 1, modes), ("row", "col", "grp"), 0, 0, tiled=True
    )
    got = lax.ppermute(give, "grp", pair)
    return pl.pallas_call(
        finish_kernel,
        out_shape=(
            jax.ShapeDtypeStruct(density.shape, f32),
            jax.ShapeDtypeStruct((depth, 1, modes), f32),
        ),
        in_specs=[vmem] * 3,
        out_specs=(hbm,) * 2,
        scratch_shapes=[pltpu.SemaphoreType.DMA((3,))],
        compiler_params=params,
        name="finish",
    )(mine, got, home)


def solution(mesh):
    in_specs = (
        P(None, None, ("row", "col"), "grp"),
        P(("row", "col"), None, "grp"),
        P(("row", "col")),
    )
    out_specs = (P(("row", "col"), None, "grp"), P(None, ("row", "col"), "grp"))
    return jax.shard_map(
        per_device, mesh=mesh, in_specs=in_specs, out_specs=out_specs, check_vma=False
    )
```

time: 33.7 us -> 31.5 us (0.935)
  waiting for transfers between devices: 6.97 us -> 4.88 us
  starting transfers between devices: 9.59 us -> 10.4 us
  other arithmetic: 0.65 us -> 0 us
  blocking collectives: 9.69 us -> 9.28 us
    ppermute x1, starting transfers between devices: 0.01 us -> 3.09 us  [per_device(): near = lax.ppermute(dens16, ('row', 'col'), even_first)]
    ppermute x1, starting transfers between devices: 7 us -> 4.35 us  [per_device(): far = lax.ppermute(dens16, ('row', 'col'), odd_first)]
    all_to_all x1, waiting for transfers between devices: 3.51 us -> 0.89 us  [per_device(): lax.all_to_all(send.reshape(2 * slabs, chunk // 4, 4, LANES), ('grp', 'ro...]
    ppermute x1, waiting for transfers between devices: 2.34 us -> 0.01 us  [per_device(): near = lax.ppermute(dens16, ('row', 'col'), even_first)]
    ppermute x1, waiting for transfers between devices: 1.12 us -> 3.3 us  [per_device(): far = lax.ppermute(dens16, ('row', 'col'), odd_first)]
    ppermute x1 -> x4, waiting for transfers between devices: 0.01 us -> 0.69 us  [the longest x1 0.68 us: per_device(): far_other = lax.ppermute(far, 'grp', pair)]
    add x1 -> x0, other arithmetic: 0.64 us -> none  [per_device(): buoyancy = (home[0] + home[1]).reshape(depth, 1, modes)]
    all_to_all x1, blocking collectives: 9.69 us -> 9.28 us  [per_device(): lax.all_to_all(back.reshape(2 * rows * owned, 1, modes), ('row', 'col', '...]
  transfers between devices with their start and end apart: 4 -> 7, of which waited for: 3 -> 3; matrix products, arithmetic and copies ran while one was open for 0% -> 0% of each run, Pallas kernels for 5% -> 6%
where the time goes in v4:
time: 31.5 us; the launch traced here: 31.2 us
  starting transfers between devices  10.4 us (33%)
  blocking collectives  9.28 us (29%)
  Pallas kernels  5.33 us (17%)
  waiting for transfers between devices  4.88 us (15%)
  between operations  1.34 us (4%)
    all_to_all x1, blocking collectives, per_device(): lax.all_to_all(back.reshape(2 * rows * owned, 1, modes), ('row', 'col', '...  9.28 us
    ppermute x1, starting transfers between devices, per_device(): far = lax.ppermute(dens16, ('row', 'col'), odd_first)  4.35 us
    ppermute x1, waiting for transfers between devices, per_device(): far = lax.ppermute(dens16, ('row', 'col'), odd_first)  3.3 us
    ppermute x1, starting transfers between devices, per_device(): near = lax.ppermute(dens16, ('row', 'col'), even_first)  3.09 us
    all_to_all x1, starting transfers between devices, per_device(): lax.all_to_all(send.reshape(2 * slabs, chunk // 4, 4, LANES), ('grp', 'ro...  2.57 us
    pallas_call x1, Pallas kernels, per_device(): pl.pallas_call(functools.partial(prepare_kernel, planes), out_shape=(jax....  2 us
    pallas_call x1, Pallas kernels, per_device(): pl.pallas_call(stencil_kernel, out_shape=(field,) * 5 + (jax.ShapeDtypeSt...  1.81 us
    all_to_all x1, waiting for transfers between devices, per_device(): lax.all_to_all(send.reshape(2 * slabs, chunk // 4, 4, LANES), ('grp', 'ro...  0.89 us
  transfers between devices with their start and end apart: 7, of which 3 were waited for; matrix products, arithmetic and copies ran while one was open for 0% of the time, Pallas kernels for 6%

profile of v4, /device:TPU:0, one launch (start us, length us, event | category | flops | bytes accessed | tf_op | source)
XLA Modules:
  0.0 31.2 jit_solution(3902685038784140806)
XLA Ops:
  0.6 2.0 %prepare.1 = (bf16[2,192,128]{2,1,0:T(8,128)(2,1)}, bf16[4,16,1024]{2,1,0:T(8,128)(2,1)S(1)}) custom-call(bf16[3,64,256]{2,1,0:T(8,128)(2,1)} %bitcast.6, f32[4,16,1024]{2,1,0:T(8,128)} %dens_hbm.3, bf16[384,384]{1,0:T(8,128)(2,1)} %constant.8.clone.mat_hbm), custom_call_target="tpu_custom_call" | custom-call | tf_op jit(solution)/shard_map/prepare/pallas_call | solution.py:233
  2.6 3.1 %collective-permute-start.1 = (bf16[4,16,1024]{2,1,0:T(8,128)(2,1)S(1)}, bf16[4,16,1024]{2,1,0:T(8,128)(2,1)S(1)}, u32[]{:S(2)}, u32[]{:S(2)}) collective-permute-start(bf16[4,16,1024]{2,1,0:T(8,128)(2,1)S(1)} %get-tuple-element.16), channel_id=1, source_target_pairs={{0,1},{1,0},{2,3},{3,2},{4,5},{5,4},{6,7},{7,6},{8,9},{9,8},{10,11... | collective-permute-start | bytes 393224 | tf_op jit(solution)/shard_map/ppermute | solution.py:256
  5.7 4.4 %collective-permute-start.2 = (bf16[4,16,1024]{2,1,0:T(8,128)(2,1)S(1)}, bf16[4,16,1024]{2,1,0:T(8,128)(2,1)S(1)}, u32[]{:S(2)}, u32[]{:S(2)}) collective-permute-start(bf16[4,16,1024]{2,1,0:T(8,128)(2,1)S(1)} %get-tuple-element.16), channel_id=1, source_target_pairs={{1,2},{2,1},{3,4},{4,3},{5,6},{6,5},{7,8},{8,7},{9,10},{10,9},{11,... | collective-permute-start | bytes 393224 | tf_op jit(solution)/shard_map/ppermute | solution.py:255
  10.1 0.0 collective-permute-start
  10.1 2.6 %all-to-all-start = ((bf16[32,3,4,128]{3,2,1,0:T(4,128)(2,1)}), bf16[32,3,4,128]{3,2,1,0:T(4,128)(2,1)S(1)}, u32[]{:S(2)}, u32[]{:S(2)}) async-start(bf16[32,3,4,128]{3,2,1,0:T(4,128)(2,1)} %bitcast.1), calls=%async_computation | async-start | bytes 196608 | tf_op jit(solution)/shard_map/all_to_all | solution.py:260
  12.7 0.0 collective-permute-done.1.near_ref
  12.7 0.3 %collective-permute-start.3 = (bf16[4,16,1024]{2,1,0:T(8,128)(2,1)S(1)}, bf16[4,16,1024]{2,1,0:T(8,128)(2,1)S(1)}, u32[]{:S(2)}, u32[]{:S(2)}) collective-permute-start(bf16[4,16,1024]{2,1,0:T(8,128)(2,1)S(1)} %collective-permute-done.1.near_ref), channel_id=1, source_target_pairs={{0,16},{16,0},{1,17},{17,1},{2,18},{18,2},{3,19},{19,3},{4,20},{20... | collective-permute-start | bytes 393224 | tf_op jit(solution)/shard_map/ppermute | solution.py:259
  13.0 3.3 %collective-permute-done.2.far_ref = bf16[4,16,1024]{2,1,0:T(8,128)(2,1)S(1)} collective-permute-done((bf16[4,16,1024]{2,1,0:T(8,128)(2,1)S(1)}, bf16[4,16,1024]{2,1,0:T(8,128)(2,1)S(1)}, u32[]{:S(2)}, u32[]{:S(2)}) %collective-permute-start.2) | collective-permute-done | bytes 131104 | tf_op jit(solution)/shard_map/ppermute | solution.py:255
  16.3 0.0 collective-permute-start.4
  16.9 0.0 collective-permute-done.3.near_other_ref
  17.0 0.7 %collective-permute-done.4.far_other_ref = bf16[4,16,1024]{2,1,0:T(8,128)(2,1)S(1)} collective-permute-done((bf16[4,16,1024]{2,1,0:T(8,128)(2,1)S(1)}, bf16[4,16,1024]{2,1,0:T(8,128)(2,1)S(1)}, u32[]{:S(2)}, u32[]{:S(2)}) %collective-permute-start.4) | collective-permute-done | bytes 131104 | tf_op jit(solution)/shard_map/ppermute | solution.py:258
  17.6 0.0 collective-permute-done.other_ref
  17.6 1.8 %stencil.1 = (f32[2,16,2048]{2,1,0:T(8,128)S(1)}, f32[2,16,2048]{2,1,0:T(8,128)S(1)}, f32[2,16,2048]{2,1,0:T(8,128)S(1)}, f32[2,16,2048]{2,1,0:T(8,128)S(1)}, f3...) custom-call(f32[4,16,1024]{2,1,0:T(8,128)} %dens_hbm.3, ...), custom_call_target="tpu_custom_call" | custom-call | flops 1048576 | bytes 1572864 | tf_op jit(solution)/shard_map/stencil/pallas_call | solution.py:266
  19.5 0.9 %all-to-all-done = bf16[32,3,4,128]{3,2,1,0:T(4,128)(2,1)S(1)} async-done(((bf16[32,3,4,128]{3,2,1,0:T(4,128)(2,1)}), bf16[32,3,4,128]{3,2,1,0:T(4,128)(2,1)S(1)}, u32[]{:S(2)}, u32[]{:S(2)}) %all-to-all-start) | async-done | bytes 98336 | tf_op jit(solution)/shard_map/all_to_all | solution.py:260
  20.3 0.8 %advance.1 = (f32[2,16,1024]{2,1,0:T(8,128)S(1)}, f32[2,16,1024]{2,1,0:T(8,128)S(1)}, f32[128,128]{1,0:T(8,128)S(1)}) custom-call(s32[1]{0:T(128)S(6)} %copy.9.live_ref, bf16[2,192,128]{2,1,0:T(8,128)(2,1)S(1)} %bitcast.4, bf16[512,1024]{1,0:T(8,128)(2,1)S(1)} %get-tuple-element.17.table_ref, f32[8,512]{1,0:T(8,128)S(1)} %get-tuple-element.18.sign_ref, ...), custom_call_target="tpu_custom_call" | custom-call | tf_op jit(solution)/shard_map/advance/pallas_call | solution.py:291
  21.1 0.1 collective-permute-start.5
  21.2 9.3 %all_to_all.10.home_ref = f32[64,1,256]{2,1,0:T(1,128)S(1)} all-to-all(f32[64,1,256]{2,1,0:T(1,128)S(1)} %bitcast.5), channel_id=1, replica_groups=mesh['grp'=2,'row'=4,'col'=4] {'row','col','grp'}, dimensions={0} | all-to-all | bytes 131072 | tf_op jit(solution)/shard_map/all_to_all | solution.py:304
  30.5 0.0 collective-permute-done.5.got_ref
  30.5 0.7 %finish.1 = (f32[4,16,1024]{2,1,0:T(8,128)}, f32[64,1,256]{2,1,0:T(1,128)}) custom-call(f32[2,16,1024]{2,1,0:T(8,128)S(1)} %get-tuple-element.25.mine_ref, f32[2,16,1024]{2,1,0:T(8,128)S(1)} %collective-permute-done.5.got_ref, f32[64,1,256]{2,1,0:T(1,128)S(1)} %all_to_all.10.home_ref), custom_call_target="tpu_custom_call" | custom-call | tf_op jit(solution)/shard_map/finish/pallas_call | solution.py:308
Async XLA Ops:
  2.6 10.0 %collective-permute-start.1 = (bf16[4,16,1024]{2,1,0:T(8,128)(2,1)S(1)}, bf16[4,16,1024]{2,1,0:T(8,128)(2,1)S(1)}, u32[]{:S(2)}, u32[]{:S(2)}) collective-permute-start(bf16[4,16,1024]{2,1,0:T(8,128)(2,1)S(1)} %get-tuple-element.16), channel_id=1, source_target_pairs={{0,1},{1,0},{2,3},{3,2},{4,5},{5,4},{6,7},{7,6},{8,9},{9,8},{10,11... | collective-permute-start | bytes 393224 | tf_op jit(solution)/shard_map/ppermute | solution.py:256
  5.7 10.6 %collective-permute-start.2 = (bf16[4,16,1024]{2,1,0:T(8,128)(2,1)S(1)}, bf16[4,16,1024]{2,1,0:T(8,128)(2,1)S(1)}, u32[]{:S(2)}, u32[]{:S(2)}) collective-permute-start(bf16[4,16,1024]{2,1,0:T(8,128)(2,1)S(1)} %get-tuple-element.16), channel_id=1, source_target_pairs={{1,2},{2,1},{3,4},{4,3},{5,6},{6,5},{7,8},{8,7},{9,10},{10,9},{11,... | collective-permute-start | bytes 393224 | tf_op jit(solution)/shard_map/ppermute | solution.py:255
  10.1 7.6 %collective-permute-start = (f32[4,16,1024]{2,1,0:T(8,128)}, f32[4,16,1024]{2,1,0:T(8,128)S(1)}, u32[]{:S(2)}, u32[]{:S(2)}) collective-permute-start(f32[4,16,1024]{2,1,0:T(8,128)} %dens_hbm.3), channel_id=1, source_target_pairs={{0,16},{16,0},{1,17},{17,1},{2,18},{18,2},{3,19},{19,3},{4,20},{20... | collective-permute-start | bytes 786440 | tf_op jit(solution)/shard_map/ppermute | solution.py:257
  10.1 10.3 %all-to-all-start = ((bf16[32,3,4,128]{3,2,1,0:T(4,128)(2,1)}), bf16[32,3,4,128]{3,2,1,0:T(4,128)(2,1)S(1)}, u32[]{:S(2)}, u32[]{:S(2)}) async-start(bf16[32,3,4,128]{3,2,1,0:T(4,128)(2,1)} %bitcast.1), calls=%async_computation | async-start | bytes 196608 | tf_op jit(solution)/shard_map/all_to_all | solution.py:260
  12.7 4.3 %collective-permute-start.3 = (bf16[4,16,1024]{2,1,0:T(8,128)(2,1)S(1)}, bf16[4,16,1024]{2,1,0:T(8,128)(2,1)S(1)}, u32[]{:S(2)}, u32[]{:S(2)}) collective-permute-start(bf16[4,16,1024]{2,1,0:T(8,128)(2,1)S(1)} %collective-permute-done.1.near_ref), channel_id=1, source_target_pairs={{0,16},{16,0},{1,17},{17,1},{2,18},{18,2},{3,19},{19,3},{4,20},{20... | collective-permute-start | bytes 393224 | tf_op jit(solution)/shard_map/ppermute | solution.py:259
  16.3 1.3 %collective-permute-start.4 = (bf16[4,16,1024]{2,1,0:T(8,128)(2,1)S(1)}, bf16[4,16,1024]{2,1,0:T(8,128)(2,1)S(1)}, u32[]{:S(2)}, u32[]{:S(2)}) collective-permute-start(bf16[4,16,1024]{2,1,0:T(8,128)(2,1)S(1)} %collective-permute-done.2.far_ref), channel_id=1, source_target_pairs={{0,16},{16,0},{1,17},{17,1},{2,18},{18,2},{3,19},{19,3},{4,20},{20... | collective-permute-start | bytes 393224 | tf_op jit(solution)/shard_map/ppermute | solution.py:258
  21.1 9.4 %collective-permute-start.5 = (f32[2,16,1024]{2,1,0:T(8,128)S(1)}, f32[2,16,1024]{2,1,0:T(8,128)S(1)}, u32[]{:S(2)}, u32[]{:S(2)}) collective-permute-start(f32[2,16,1024]{2,1,0:T(8,128)S(1)} %get-tuple-element.26), channel_id=1, source_target_pairs={{0,16},{16,0},{1,17},{17,1},{2,18},{18,2},{3,19},{19,3},{4,20},{20... | collective-permute-start | bytes 393224 | tf_op jit(solution)/shard_map/ppermute | solution.py:307

commit v5 on v4

--- a/solution.py
+++ b/solution.py
@@ -58,17 +58,32 @@
 
 
 def prepare_kernel(
-    planes, vel_hbm, dens_hbm, mat_hbm, send_ref, dens16_ref, vel_ref, dens_ref, mat_ref, sems
+    planes, vel_hbm, dens_hbm, mat_hbm,
+    send_hbm, dens16_ref, dens_ref, give_ref, vel_ref, mat_ref, send_ref, sems,
 ):
     copies = copy_all([(dens_hbm, dens_ref), (vel_hbm, vel_ref), (mat_hbm, mat_ref)], sems)
+    copies[0].wait()
+    dens16_ref[...] = dens_ref[...].astype(jnp.bfloat16)
+    owned = planes // 2
+    give_ref[...] = dens_ref[pl.ds(owned * (1 - lax.axis_index("grp")), owned)]
+    copies[1].wait()
+    copies[2].wait()
+    pl.when(lax.axis_index("col") == 0)(
+        lambda: order_velocity(planes, vel_ref, mat_ref, send_ref, send_hbm, sems.at[0])
+    )
+
+
+def order_kernel(planes, vel_ref, mat_ref, unused_hbm, send_hbm, send_ref, sem):
+    pl.when(lax.axis_index("col") != 0)(
+        lambda: order_velocity(planes, vel_ref, mat_ref, send_ref, send_hbm, sem)
+    )
+
+
+def order_velocity(planes, vel_ref, mat_ref, send_ref, send_hbm, sem):
     comps, depth, modes = vel_ref.shape
     tiles = modes // LANES
     step = GROUP * planes
     chunk = comps * planes * tiles * GROUP // 2
-    copies[0].wait()
-    dens16_ref[...] = dens_ref[...].astype(jnp.bfloat16)
-    copies[1].wait()
-    copies[2].wait()
     for b in range(depth // step):
         parts = []
         for c in range(comps):
@@ -78,78 +93,90 @@
         mixed = exact(mat_ref[...], jnp.concatenate(parts, axis=0))
         for g in range(2):
             send_ref[g, pl.ds(b * chunk, chunk), :] = mixed[g * chunk : (g + 1) * chunk]
-
-
-def stencil_kernel(
-    dens_hbm, other_ref, near_ref, far_ref, near_other_ref, far_other_ref,
-    table_hbm, sign_hbm, in_hbm,
-    gx_ref, gy_ref, gz_ref, base_ref, field_ref, table_ref, sign_ref, in_ref, zz_ref, sems,
+    copy = pltpu.make_async_copy(send_ref, send_hbm, sem)
+    copy.start()
+    copy.wait()
+
+
+def local_kernel(
+    dens_ref, other_ref, live_ref, table_hbm, sign_hbm, in_hbm,
+    gx_ref, gy_ref, base_ref, mask_ref, table_ref, sign_ref, in_ref, sems,
 ):
-    planes, rows, cells = dens_hbm.shape
-    here, there = pl.ds(0, cells), pl.ds(cells, cells)
+    planes, rows, cells = dens_ref.shape
     core = lax.axis_index("grp")
     copies = copy_all(
-        [
-            (dens_hbm, zz_ref.at[pl.ds(planes, planes), :, here]),
-            (table_hbm.at[core], table_ref), (sign_hbm, sign_ref), (in_hbm, in_ref),
-        ],
-        sems,
-    )
-    zz_ref[pl.ds(planes, planes), :, there] = other_ref[...]
+        [(table_hbm.at[core], table_ref), (sign_hbm, sign_ref), (in_hbm, in_ref)], sems
+    )
+    owned = planes // 2
+
+    def one(p):
+        at = owned * core + p
+        field = jnp.concatenate([dens_ref[at], other_ref[p]], axis=1)
+        live = (at < live_ref[0]).astype(jnp.float32)
+        grad_x, grad_y, lap = differences(
+            lambda m: pltpu.roll(field, (-m) % (2 * cells), 1),
+            lambda m: pltpu.roll(field, (-m) % rows, 0),
+        )
+        mask_ref[p] = jnp.broadcast_to(live, mask_ref.shape[1:])
+        gx_ref[p] = live * grad_x
+        gy_ref[p] = live * grad_y
+        base_ref[p] = field + live * (
+            (step_value * kappa_value * 3.0 * centre_coef) * field + lap
+        )
+
+    loop_planes(owned, rows, one)
+    for copy in copies:
+        copy.wait()
+
+
+def halo_kernel(far_ref, near_ref, dens_ref, mine_ref, give_ref, zz_ref):
+    planes = dens_ref.shape[0]
     odd = lax.axis_index(("row", "col")) % 2
-    near_at, far_at = pl.ds(2 * planes * (1 - odd), planes), pl.ds(2 * planes * odd, planes)
-    zz_ref[near_at, :, here] = near_ref[...].astype(jnp.float32)
-    zz_ref[near_at, :, there] = near_other_ref[...].astype(jnp.float32)
-    zz_ref[far_at, :, here] = far_ref[...].astype(jnp.float32)
-    zz_ref[far_at, :, there] = far_other_ref[...].astype(jnp.float32)
-    copies[0].wait()
-    span = 2 * cells
+    zz_ref[pl.ds(2 * planes * (1 - odd), planes)] = near_ref[...].astype(jnp.float32)
+    zz_ref[pl.ds(2 * planes * odd, planes)] = far_ref[...].astype(jnp.float32)
+    zz_ref[pl.ds(planes, planes)] = dens_ref[...]
     owned = planes // 2
-
-    def one(p):
-        at = planes + owned * core + p
-        field = zz_ref[at]
-        field_ref[p] = field
-        grad_x = grad_y = grad_z = lap = None
-        for reach in range(1, 5):
-            ahead_x = pltpu.roll(field, span - reach, 1)
-            behind_x = pltpu.roll(field, reach, 1)
-            ahead_y = pltpu.roll(field, rows - reach, 0)
-            behind_y = pltpu.roll(field, reach, 0)
-            ahead_z = zz_ref[at + reach]
-            behind_z = zz_ref[at - reach]
-            a = step_value * first_coef[reach - 1]
-            b = step_value * kappa_value * second_coef[reach - 1]
-            total = (ahead_x + behind_x) + (ahead_y + behind_y) + (ahead_z + behind_z)
-            if reach == 1:
-                grad_x = a * (ahead_x - behind_x)
-                grad_y = a * (ahead_y - behind_y)
-                grad_z = a * (ahead_z - behind_z) + step_value * strat_value
-                lap = (1.0 + step_value * kappa_value * 3.0 * centre_coef) * field + b * total
-            else:
-                grad_x = grad_x + a * (ahead_x - behind_x)
-                grad_y = grad_y + a * (ahead_y - behind_y)
-                grad_z = grad_z + a * (ahead_z - behind_z)
-                lap = lap + b * total
-        gx_ref[p] = grad_x
-        gy_ref[p] = grad_y
-        gz_ref[p] = grad_z
-        base_ref[p] = lap
-
+    core = lax.axis_index("grp")
+
+    for out_ref, first in ((mine_ref, owned * core), (give_ref, owned * (1 - core))):
+
+        def one(p):
+            grad_z, lap = differences(lambda m: zz_ref[planes + first + p + m])
+            out_ref[0, p] = (grad_z + step_value * strat_value).astype(out_ref.dtype)
+            out_ref[1, p] = lap.astype(out_ref.dtype)
+
+        loop_planes(owned, dens_ref.shape[1], one)
+
+
+def differences(*shifted):
+    grads = [None] * len(shifted)
+    lap = None
+    for reach in range(1, 5):
+        a = step_value * first_coef[reach - 1]
+        b = step_value * kappa_value * second_coef[reach - 1]
+        total = None
+        for i, shift in enumerate(shifted):
+            ahead, behind = shift(reach), shift(-reach)
+            grad, pair = a * (ahead - behind), ahead + behind
+            grads[i] = grad if reach == 1 else grads[i] + grad
+            total = pair if total is None else total + pair
+        lap = b * total if reach == 1 else lap + b * total
+    return (*grads, lap)
+
+
+def loop_planes(count, rows, body):
     if rows <= GROUP:
-        for p in range(owned):
-            one(p)
+        for p in range(count):
+            body(p)
     else:
-        lax.fori_loop(0, owned, lambda p, _: (one(p), 0)[1], 0)
-    for copy in copies[1:]:
-        copy.wait()
+        lax.fori_loop(0, count, lambda p, _: (body(p), 0)[1], 0)
 
 
 def advance_kernel(
-    scale, live_ref, recv_ref, table_ref, sign_ref, in_mat_ref,
-    dens_ref, gx_ref, gy_ref, gz_ref, base_ref, mine_ref, give_ref, send_ref, fine_ref,
+    scale, recv_ref, table_ref, sign_ref, in_mat_ref, gx_ref, gy_ref, base_ref, mask_ref,
+    z_mine_ref, z_other_ref, mine_ref, give_ref, send_ref, fine_ref,
 ):
-    owned, rows, span = dens_ref.shape
+    owned, rows, span = base_ref.shape
     cells = span // 2
     modes = table_ref.shape[0]
     tiles = modes // (2 * LANES)
@@ -157,7 +184,6 @@
     chunk = comps * owned * tiles * GROUP
     per_tile = chunk // tiles
     sign = sign_ref[0:1, :]
-    first_plane = owned * lax.axis_index("grp")
     for b in range(rows // GROUP):
         lanes = [recv_ref[g, pl.ds(b * chunk, chunk), :] for g in range(2)]
         mixed = jnp.dot(
@@ -170,17 +196,21 @@
         fine_ref[...] = jnp.dot(both, table_ref[...], preferred_element_type=jnp.float32)
         here = pl.ds(b * GROUP, GROUP)
         parts = []
-        for side, out_ref in enumerate((mine_ref, give_ref)):
+        for side, (out_ref, z_ref) in enumerate(
+            ((mine_ref, z_mine_ref), (give_ref, z_other_ref))
+        ):
             for p in range(owned):
                 at = (p, here, pl.ds(side * cells, cells))
                 vel = [
                     fine_ref[pl.ds(((side * comps + c) * owned + p) * GROUP, GROUP), :]
                     for c in range(comps)
                 ]
-                moved = base_ref[at] - (
-                    vel[0] * gx_ref[at] + vel[1] * gy_ref[at] + vel[2] * gz_ref[at]
+                grad_z, lap_z = (z_ref[i, p, here, :].astype(jnp.float32) for i in range(2))
+                along_z = vel[2] * grad_z - lap_z
+                value = base_ref[at] - (
+                    vel[0] * gx_ref[at] + vel[1] * gy_ref[at]
+                    + mask_ref[p, :, pl.ds(side * cells, cells)] * along_z
                 )
-                value = jnp.where(first_plane + p < live_ref[0], moved, dens_ref[at])
                 out_ref[p, here, :] = value
                 parts.append(value.astype(jnp.bfloat16))
         lifted = lax.dot_general(
@@ -230,76 +260,94 @@
     params = pltpu.CompilerParams(vmem_limit_bytes=(24 if rows <= GROUP else 56) * 2**20)
     f32, b16 = jnp.float32, jnp.bfloat16
 
-    send, dens16 = pl.pallas_call(
+    half_field = jax.ShapeDtypeStruct((owned, rows, cells), f32)
+    send_shape = (2, slabs * chunk, LANES)
+    send, dens16, dens, give, vel, mat = pl.pallas_call(
         functools.partial(prepare_kernel, planes),
         out_shape=(
-            jax.ShapeDtypeStruct((2, slabs * chunk, LANES), b16),
+            pltpu.HBM(send_shape, b16),
             jax.ShapeDtypeStruct(density.shape, b16),
+            jax.ShapeDtypeStruct(density.shape, f32),
+            half_field,
+            jax.ShapeDtypeStruct((comps, depth, modes), b16),
+            jax.ShapeDtypeStruct(prep_mat.shape, b16),
         ),
         in_specs=[hbm] * 3,
-        out_specs=(vmem,) * 2,
-        scratch_shapes=[
-            pltpu.VMEM((comps, depth, modes), b16),
-            pltpu.VMEM(density.shape, f32),
-            pltpu.VMEM(prep_mat.shape, b16),
-            pltpu.SemaphoreType.DMA((3,)),
-        ],
+        out_specs=(hbm,) + (vmem,) * 5,
+        scratch_shapes=[pltpu.VMEM(send_shape, b16), pltpu.SemaphoreType.DMA((3,))],
         compiler_params=params,
         name="prepare",
     )(keep(velocity.reshape(comps, depth, modes)), keep(density), keep(prep_mat))
+    send = pl.pallas_call(
+        functools.partial(order_kernel, planes),
+        out_shape=jax.ShapeDtypeStruct(send_shape, b16),
+        in_specs=[vmem, vmem, hbm],
+        out_specs=hbm,
+        input_output_aliases={2: 0},
+        scratch_shapes=[pltpu.VMEM(send_shape, b16), pltpu.SemaphoreType.DMA],
+        compiler_params=params,
+        name="order",
+    )(vel, mat, keep(send))
 
     count = slabs
     even_first = [(i, i ^ 1) for i in range(count)]
     odd_first = [((i + 1) % count, ((i ^ 1) + 1) % count) for i in range(count)]
     pair = [(0, 1), (1, 0)]
+    near = lax.ppermute(dens16, ("row", "col"), even_first)
     far = lax.ppermute(dens16, ("row", "col"), odd_first)
-    near = lax.ppermute(dens16, ("row", "col"), even_first)
-    other = lax.ppermute(density, "grp", pair)
-    far_other = lax.ppermute(far, "grp", pair)
-    near_other = lax.ppermute(near, "grp", pair)
+    other = lax.ppermute(give, "grp", pair)
     recv = lax.all_to_all(
         send.reshape(2 * slabs, chunk // 4, 4, LANES), ("grp", "row", "col"), 0, 0, tiled=True
     )
     recv = recv.reshape(2, slabs * chunk, LANES)
 
+    z_shape = (2, owned, rows, cells)
+    z_mine, z_give = pl.pallas_call(
+        halo_kernel,
+        out_shape=(jax.ShapeDtypeStruct(z_shape, f32), jax.ShapeDtypeStruct(z_shape, b16)),
+        in_specs=[vmem] * 3,
+        out_specs=(vmem,) * 2,
+        scratch_shapes=[pltpu.VMEM((3 * planes, rows, cells), f32)],
+        compiler_params=params,
+        cost_estimate=pl.CostEstimate(
+            flops=16 * density.size, bytes_accessed=16 * density.size, transcendentals=0
+        ),
+        name="halo",
+    )(far, near, dens)
+    z_other = lax.ppermute(z_give, "grp", pair)
+
     field = jax.ShapeDtypeStruct((owned, rows, fine_cells), f32)
-    *grads, table, sign, in_mat = pl.pallas_call(
-        stencil_kernel,
-        out_shape=(field,) * 5 + (
+    gx, gy, base, mask, table, sign, in_mat = pl.pallas_call(
+        local_kernel,
+        out_shape=(field,) * 3 + (
+            jax.ShapeDtypeStruct((owned, 1, fine_cells), f32),
             jax.ShapeDtypeStruct(tables[0].shape, b16),
             jax.ShapeDtypeStruct(sign.shape, f32),
             jax.ShapeDtypeStruct(in_mat.shape, b16),
         ),
-        in_specs=[hbm] + [vmem] * 5 + [hbm] * 3,
-        out_specs=(vmem,) * 8,
-        scratch_shapes=[
-            pltpu.VMEM((3 * planes, rows, fine_cells), f32), pltpu.SemaphoreType.DMA((4,))
-        ],
+        in_specs=[vmem, vmem, smem] + [hbm] * 3,
+        out_specs=(vmem,) * 7,
+        scratch_shapes=[pltpu.SemaphoreType.DMA((3,))],
         compiler_params=params,
         cost_estimate=pl.CostEstimate(
             flops=16 * density.size, bytes_accessed=24 * density.size, transcendentals=0
         ),
-        name="stencil",
-    )(
-        keep(density), other, near, far, near_other, far_other,
-        keep(tables), keep(sign), keep(in_mat),
-    )
-    gx, gy, gz, base, dens = grads
+        name="local",
+    )(dens, other, live_planes, keep(tables), keep(sign), keep(in_mat))
 
     scale = -math.sqrt(2.0 / fine_cells)
-    half_field = jax.ShapeDtypeStruct((owned, rows, cells), f32)
     mine, give, back = pl.pallas_call(
         functools.partial(advance_kernel, scale),
         out_shape=(
             half_field, half_field,
             jax.ShapeDtypeStruct((rows * 2 * owned * tiles, LANES), f32),
         ),
-        in_specs=[smem] + [vmem] * 9,
+        in_specs=[vmem] * 10,
         out_specs=(vmem,) * 3,
         scratch_shapes=[pltpu.VMEM((2 * comps * owned * GROUP, cells), f32)],
         compiler_params=params,
         name="advance",
-    )(live_planes, recv, table, sign, in_mat, dens, gx, gy, gz, base)
+    )(recv, table, sign, in_mat, gx, gy, base, mask, z_mine, z_other)
 
     home = lax.all_to_all(
         back.reshape(2 * rows * owned, 1, modes), ("row", "col", "grp"), 0, 0, tiled=True

time: 31.5 us -> 30.7 us (0.975)
  starting transfers between devices: 10.4 us -> 9.62 us
  waiting for transfers between devices: 4.88 us -> 4.5 us
  Pallas kernels: 5.33 us -> 5.68 us
    ppermute x1, starting transfers between devices: 3.09 us -> 2.21 us  [per_device(): near = lax.ppermute(dens16, ('row', 'col'), even_first)]
    ppermute x3 -> x2, waiting for transfers between devices: 0.69 us -> 0.01 us  [the longest x1 0.01 us: per_device(): other = lax.ppermute(give, 'grp', pair)]
    all_to_all x1, waiting for transfers between devices: 0.89 us -> 1.24 us  [per_device(): lax.all_to_all(send.reshape(2 * slabs, chunk // 4, 4, LANES), ('grp', 'ro...]
    pallas_call x2 -> x4, Pallas kernels: 3.8 us -> 4.14 us  [the longest x1 2 us: per_device(): pl.pallas_call(functools.partial(prepare_kernel, planes), out_shape=(pltp...]
  transfers between devices with their start and end apart: 7 -> 6, of which waited for: 3 -> 2; matrix products, arithmetic and copies ran while one was open for 0% -> 0% of each run, Pallas kernels for 6% -> 7%
where the time goes in v5:
time: 30.7 us; the launch traced here: 30.4 us
  starting transfers between devices  9.62 us (31%)
  blocking collectives  9.29 us (30%)
  Pallas kernels  5.68 us (19%)
  waiting for transfers between devices  4.5 us (15%)
  between operations  1.34 us (4%)
    all_to_all x1, blocking collectives, per_device(): lax.all_to_all(back.reshape(2 * rows * owned, 1, modes), ('row', 'col', '...  9.29 us
    ppermute x1, starting transfers between devices, per_device(): far = lax.ppermute(dens16, ('row', 'col'), odd_first)  4.36 us
    ppermute x1, waiting for transfers between devices, per_device(): far = lax.ppermute(dens16, ('row', 'col'), odd_first)  3.25 us
    all_to_all x1, starting transfers between devices, per_device(): lax.all_to_all(send.reshape(2 * slabs, chunk // 4, 4, LANES), ('grp', 'ro...  2.6 us
    ppermute x1, starting transfers between devices, per_device(): near = lax.ppermute(dens16, ('row', 'col'), even_first)  2.21 us
    pallas_call x1, Pallas kernels, per_device(): pl.pallas_call(functools.partial(prepare_kernel, planes), out_shape=(pltp...  2 us
    pallas_call x1, Pallas kernels, per_device(): pl.pallas_call(local_kernel, out_shape=(field,) * 3 + (jax.ShapeDtypeStru...  1.8 us
    all_to_all x1, waiting for transfers between devices, per_device(): lax.all_to_all(send.reshape(2 * slabs, chunk // 4, 4, LANES), ('grp', 'ro...  1.24 us
  transfers between devices with their start and end apart: 6, of which 2 were waited for; matrix products, arithmetic and copies ran while one was open for 0% of the time, Pallas kernels for 7%

profile of v5, /device:TPU:0, one launch (start us, length us, event | category | flops | bytes accessed | tf_op | source)
XLA Modules:
  0.0 30.4 jit_solution(14864706472092443788)
XLA Ops:
  0.6 2.0 %prepare.1 = (bf16[2,192,128]{2,1,0:T(8,128)(2,1)}, bf16[4,16,1024]{2,1,0:T(8,128)(2,1)S(1)}, f32[4,16,1024]{2,1,0:T(8,128)S(1)}, f32[2,16,1024]{2,1,0:T(8,128)S...) custom-call(bf16[3,64,256]{2,1,0:T(8,128)(2,1)} %bitcast.7, f32[4,16,1024]{2,1,0:T(8,128)} %dens_hbm.1, ...), custom_call_target="tpu_custom_call" | custom-call | tf_op jit(solution)/shard_map/prepare/pallas_call | solution.py:265
  2.6 2.2 %collective-permute-start.2 = (bf16[4,16,1024]{2,1,0:T(8,128)(2,1)S(1)}, bf16[4,16,1024]{2,1,0:T(8,128)(2,1)S(1)}, u32[]{:S(2)}, u32[]{:S(2)}) collective-permute-start(bf16[4,16,1024]{2,1,0:T(8,128)(2,1)S(1)} %get-tuple-element.32), channel_id=1, source_target_pairs={{0,1},{1,0},{2,3},{3,2},{4,5},{5,4},{6,7},{7,6},{8,9},{9,8},{10,11... | collective-permute-start | bytes 393224 | tf_op jit(solution)/shard_map/ppermute | solution.py:296
  4.8 4.4 %collective-permute-start.1 = (bf16[4,16,1024]{2,1,0:T(8,128)(2,1)S(1)}, bf16[4,16,1024]{2,1,0:T(8,128)(2,1)S(1)}, u32[]{:S(2)}, u32[]{:S(2)}) collective-permute-start(bf16[4,16,1024]{2,1,0:T(8,128)(2,1)S(1)} %get-tuple-element.32), channel_id=1, source_target_pairs={{1,2},{2,1},{3,4},{4,3},{5,6},{6,5},{7,8},{8,7},{9,10},{10,9},{11,... | collective-permute-start | bytes 393224 | tf_op jit(solution)/shard_map/ppermute | solution.py:297
  9.2 2.6 %all-to-all-start = ((bf16[32,3,4,128]{3,2,1,0:T(4,128)(2,1)}), bf16[32,3,4,128]{3,2,1,0:T(4,128)(2,1)S(1)}, u32[]{:S(2)}, u32[]{:S(2)}) async-start(bf16[32,3,4,128]{3,2,1,0:T(4,128)(2,1)} %bitcast.6), calls=%async_computation | async-start | bytes 196608 | tf_op jit(solution)/shard_map/all_to_all | solution.py:299
  11.8 0.3 %collective-permute-start = (f32[2,16,1024]{2,1,0:T(8,128)S(1)}, f32[2,16,1024]{2,1,0:T(8,128)S(1)}, u32[]{:S(2)}, u32[]{:S(2)}) collective-permute-start(f32[2,16,1024]{2,1,0:T(8,128)S(1)} %get-tuple-element.24), channel_id=1, source_target_pairs={{0,16},{16,0},{1,17},{17,1},{2,18},{18,2},{3,19},{19,3},{4,20},{20... | collective-permute-start | bytes 393224 | tf_op jit(solution)/shard_map/ppermute | solution.py:298
  12.1 0.0 collective-permute-done.2.near_ref
  12.1 3.2 %collective-permute-done.1.far_ref = bf16[4,16,1024]{2,1,0:T(8,128)(2,1)S(1)} collective-permute-done((bf16[4,16,1024]{2,1,0:T(8,128)(2,1)S(1)}, bf16[4,16,1024]{2,1,0:T(8,128)(2,1)S(1)}, u32[]{:S(2)}, u32[]{:S(2)}) %collective-permute-start.1) | collective-permute-done | bytes 131104 | tf_op jit(solution)/shard_map/ppermute | solution.py:297
  15.4 0.3 %halo.1 = (f32[2,2,16,1024]{3,2,1,0:T(8,128)S(1)}, bf16[2,2,16,1024]{3,2,1,0:T(8,128)(2,1)S(1)}) custom-call(bf16[4,16,1024]{2,1,0:T(8,128)(2,1)S(1)} %collective-permute-done.1.far_ref, bf16[4,16,1024]{2,1,0:T(8,128)(2,1)S(1)} %collective-permute-done.2.near_ref, f32[4,16,1024]{2,1,0:T(8,128)S(1)} %get-tuple-element.23.dens_ref), custom_call_target="tpu_custom_call" | custom-call | flops 1048576 | bytes 1048576 | tf_op jit(solution)/shard_map/halo/pallas_call | solution.py:305
  15.7 0.1 collective-permute-start.3
  16.5 0.0 collective-permute-done.other_ref
  16.5 1.8 %local.1 = (f32[2,16,2048]{2,1,0:T(8,128)S(1)}, f32[2,16,2048]{2,1,0:T(8,128)S(1)}, f32[2,16,2048]{2,1,0:T(8,128)S(1)}, f32[2,1,2048]{2,1,0:T(1,128)S(1)}, bf16[...) custom-call(f32[4,16,1024]{2,1,0:T(8,128)S(1)} %get-tuple-element.23.dens_ref, ...), custom_call_target="tpu_custom_call" | custom-call | flops 1048576 | bytes 1572864 | tf_op jit(solution)/shard_map/local/pallas_call | solution.py:320
  18.3 1.2 %all-to-all-done = bf16[32,3,4,128]{3,2,1,0:T(4,128)(2,1)S(1)} async-done(((bf16[32,3,4,128]{3,2,1,0:T(4,128)(2,1)}), bf16[32,3,4,128]{3,2,1,0:T(4,128)(2,1)S(1)}, u32[]{:S(2)}, u32[]{:S(2)}) %all-to-all-start) | async-done | bytes 98336 | tf_op jit(solution)/shard_map/all_to_all | solution.py:299
  19.5 0.0 collective-permute-done.3.z_other_ref
  19.5 0.8 %advance.1 = (f32[2,16,1024]{2,1,0:T(8,128)S(1)}, f32[2,16,1024]{2,1,0:T(8,128)S(1)}, f32[128,128]{1,0:T(8,128)S(1)}) custom-call(bf16[2,192,128]{2,1,0:T(8,128)(2,1)S(1)} %bitcast.4, bf16[512,1024]{1,0:T(8,128)(2,1)S(1)} %get-tuple-element.25.table_ref, f32[8,512]{1,0:T(8,128)S(1)} %get-tuple-element.26.sign_ref, ...), custom_call_target="tpu_custom_call" | custom-call | tf_op jit(solution)/shard_map/advance/pallas_call | solution.py:339
  20.3 0.1 collective-permute-start.4
  20.4 9.3 %all_to_all.10.home_ref = f32[64,1,256]{2,1,0:T(1,128)S(1)} all-to-all(f32[64,1,256]{2,1,0:T(1,128)S(1)} %bitcast.5), channel_id=1, replica_groups=mesh['grp'=2,'row'=4,'col'=4] {'row','col','grp'}, dimensions={0} | all-to-all | bytes 131072 | tf_op jit(solution)/shard_map/all_to_all | solution.py:352
  29.7 0.0 collective-permute-done.4.got_ref
  29.7 0.7 %finish.1 = (f32[4,16,1024]{2,1,0:T(8,128)}, f32[64,1,256]{2,1,0:T(1,128)}) custom-call(f32[2,16,1024]{2,1,0:T(8,128)S(1)} %get-tuple-element.35.mine_ref, f32[2,16,1024]{2,1,0:T(8,128)S(1)} %collective-permute-done.4.got_ref, f32[64,1,256]{2,1,0:T(1,128)S(1)} %all_to_all.10.home_ref), custom_call_target="tpu_custom_call" | custom-call | tf_op jit(solution)/shard_map/finish/pallas_call | solution.py:356
  (1 shorter events, 0.0 us)
Async XLA Ops:
  2.6 9.5 %collective-permute-start.2 = (bf16[4,16,1024]{2,1,0:T(8,128)(2,1)S(1)}, bf16[4,16,1024]{2,1,0:T(8,128)(2,1)S(1)}, u32[]{:S(2)}, u32[]{:S(2)}) collective-permute-start(bf16[4,16,1024]{2,1,0:T(8,128)(2,1)S(1)} %get-tuple-element.32), channel_id=1, source_target_pairs={{0,1},{1,0},{2,3},{3,2},{4,5},{5,4},{6,7},{7,6},{8,9},{9,8},{10,11... | collective-permute-start | bytes 393224 | tf_op jit(solution)/shard_map/ppermute | solution.py:296
  4.8 10.5 %collective-permute-start.1 = (bf16[4,16,1024]{2,1,0:T(8,128)(2,1)S(1)}, bf16[4,16,1024]{2,1,0:T(8,128)(2,1)S(1)}, u32[]{:S(2)}, u32[]{:S(2)}) collective-permute-start(bf16[4,16,1024]{2,1,0:T(8,128)(2,1)S(1)} %get-tuple-element.32), channel_id=1, source_target_pairs={{1,2},{2,1},{3,4},{4,3},{5,6},{6,5},{7,8},{8,7},{9,10},{10,9},{11,... | collective-permute-start | bytes 393224 | tf_op jit(solution)/shard_map/ppermute | solution.py:297
  9.2 10.3 %all-to-all-start = ((bf16[32,3,4,128]{3,2,1,0:T(4,128)(2,1)}), bf16[32,3,4,128]{3,2,1,0:T(4,128)(2,1)S(1)}, u32[]{:S(2)}, u32[]{:S(2)}) async-start(bf16[32,3,4,128]{3,2,1,0:T(4,128)(2,1)} %bitcast.6), calls=%async_computation | async-start | bytes 196608 | tf_op jit(solution)/shard_map/all_to_all | solution.py:299
  11.8 4.6 %collective-permute-start = (f32[2,16,1024]{2,1,0:T(8,128)S(1)}, f32[2,16,1024]{2,1,0:T(8,128)S(1)}, u32[]{:S(2)}, u32[]{:S(2)}) collective-permute-start(f32[2,16,1024]{2,1,0:T(8,128)S(1)} %get-tuple-element.24), channel_id=1, source_target_pairs={{0,16},{16,0},{1,17},{17,1},{2,18},{18,2},{3,19},{19,3},{4,20},{20... | collective-permute-start | bytes 393224 | tf_op jit(solution)/shard_map/ppermute | solution.py:298
  15.7 3.8 %collective-permute-start.3 = (bf16[2,2,16,1024]{3,2,1,0:T(8,128)(2,1)S(1)}, bf16[2,2,16,1024]{3,2,1,0:T(8,128)(2,1)S(1)}, u32[]{:S(2)}, u32[]{:S(2)}) collective-permute-start(bf16[2,2,16,1024]{3,2,1,0:T(8,128)(2,1)S(1)} %get-tuple-element.34), channel_id=1, source_target_pairs={{0,16},{16,0},{1,17},{17,1},{2,18},{18,2},{3,19},{19,3},{4,20},{20... | collective-permute-start | bytes 393224 | tf_op jit(solution)/shard_map/ppermute | solution.py:317
  20.3 9.4 %collective-permute-start.4 = (f32[2,16,1024]{2,1,0:T(8,128)S(1)}, f32[2,16,1024]{2,1,0:T(8,128)S(1)}, u32[]{:S(2)}, u32[]{:S(2)}) collective-permute-start(f32[2,16,1024]{2,1,0:T(8,128)S(1)} %get-tuple-element.36), channel_id=1, source_target_pairs={{0,16},{16,0},{1,17},{17,1},{2,18},{18,2},{3,19},{19,3},{4,20},{20... | collective-permute-start | bytes 393224 | tf_op jit(solution)/shard_map/ppermute | solution.py:355
